TPU v7x, 32 devices: a whole 2x2x4 slice. The times are simulated.
32 devices in a mesh: dp: 4 (over y, core), fsdp: 8 (over z, x).
Axes of the slice: x: 2, y: 2, z: 4, core: 2. Of those that a mesh axis runs over, the one named last changes fastest.
Arguments:
- tokens: bfloat16 [32768, 1024], P(('dp', 'fsdp')), may hold values from -6 to 6
- doc_ids: int32 [32, 1024], P(('dp', 'fsdp')), may hold values from 0 to 7, never falling along the last dimension, each value on 1 to 512 neighbouring positions
- norm_in: bfloat16 [1024], P(('dp', 'fsdp')), may hold values from 0.25 to 1.75
- query_weight: bfloat16 [1024, 1024], P(('dp', 'fsdp')), may hold values from -0.1875 to 0.1875
- latent_weight: bfloat16 [1024, 512], P(('dp', 'fsdp')), may hold values from -0.1875 to 0.1875
- key_up_weight: bfloat16 [512, 512], P(('dp', 'fsdp')), may hold values from -0.375 to 0.375
- value_up_weight: bfloat16 [512, 512], P(('dp', 'fsdp')), may hold values from -0.375 to 0.375
- output_weight: bfloat16 [1024, 1024], P(('dp', 'fsdp')), may hold values from -1.5 to 1.5
- norm_mid: bfloat16 [1024], P(('dp', 'fsdp')), may hold values from 0.25 to 1.75
- gate_weight: bfloat16 [1024, 2816], P(('dp', 'fsdp')), may hold values from -0.1875 to 0.1875
- up_weight: bfloat16 [1024, 2816], P(('dp', 'fsdp')), may hold values from -0.1875 to 0.1875
- down_weight: bfloat16 [2816, 1024], P(('dp', 'fsdp')), may hold values from -0.109375 to 0.109375
- cotangent: bfloat16 [32768, 1024], P(('dp', 'fsdp')), may hold values from -6 to 6
Outputs:
- layer_out: bfloat16 [32768, 1024], P(('dp', 'fsdp'))
- grad_tokens: bfloat16 [32768, 1024], P(('dp', 'fsdp'))
- grad_norm_in: float32 [1024], P(('dp', 'fsdp'))
- grad_query: float32 [1024, 1024], P(('dp', 'fsdp'))
- grad_latent: float32 [1024, 512], P(('dp', 'fsdp'))
- grad_key_up: float32 [512, 512], P(('dp', 'fsdp'))
- grad_value_up: float32 [512, 512], P(('dp', 'fsdp'))
- grad_output: float32 [1024, 1024], P(('dp', 'fsdp'))
- grad_norm_mid: float32 [1024], P(('dp', 'fsdp'))
- grad_gate: float32 [1024, 2816], P(('dp', 'fsdp'))
- grad_up: float32 [1024, 2816], P(('dp', 'fsdp'))
- grad_down: float32 [2816, 1024], P(('dp', 'fsdp'))
Inputs may be any that keep to these rules, and one draw needn't show every extreme that they name: `doc_ids`: along each row of 1024 tokens the ids never fall; a document has 1 to 512 tokens of a row.
All inputs are finite; a program needn't handle non-finite values.
Results may differ from a plain program's by a relative error of at most 0.017.
Values may be sent and summed in bfloat16 or wider, within the bound.
No kernel may reach another device: no remote copies, remote signals or barrier semaphores. Data moves between devices by JAX's collectives and lax.ppermute only.
A program may use at most 256 MiB of HBM per device.

v0:
```python
import jax
import jax.numpy as jnp
from jax import lax
from jax.sharding import PartitionSpec as P

HD = 64
G = 2
HG = 8


EPSILON = 1e-05
SCORE_SCALE = 0.125
NEGATIVE = -1e30


def rms_parts(values, gain):
    inv_root = lax.rsqrt(jnp.mean(values * values, axis=-1, keepdims=True) + EPSILON)
    unit_rows = values * inv_root
    return (unit_rows * gain, unit_rows, inv_root)


def rms_back(grad_outer, unit_rows, inv_root, gain):
    grad_unit = grad_outer * gain
    grad_gain = jnp.sum(grad_outer * unit_rows, axis=0)
    inner_mean = jnp.mean(grad_unit * unit_rows, axis=-1, keepdims=True)
    return (inv_root * (grad_unit - unit_rows * inner_mean), grad_gain)


def latent_up(latents, weight):
    token_count = latents.shape[0]
    latent_groups = latents.reshape(token_count, G, -1)
    weight_groups = weight.reshape(G, latent_groups.shape[2], -1)
    return jnp.einsum(
        "ngl,glf->ngf", latent_groups, weight_groups, preferred_element_type=jnp.float32
    ).reshape(token_count, -1)


def latent_back(latents, weight, grad_heads):
    token_count = latents.shape[0]
    latent_groups = latents.reshape(token_count, G, -1)
    weight_groups = weight.reshape(G, latent_groups.shape[2], -1)
    grad_groups = grad_heads.reshape(token_count, G, -1)
    grad_weight = jnp.einsum(
        "ngl,ngf->glf", latent_groups, grad_groups, preferred_element_type=jnp.float32
    )
    grad_latents = jnp.einsum(
        "ngf,glf->ngl", grad_groups, weight_groups, preferred_element_type=jnp.float32
    )
    return (grad_weight.reshape(weight.shape), grad_latents.reshape(token_count, -1))


def block_visible(doc_row, start_row, block_rows):
    length = doc_row.shape[0]
    doc_block = lax.dynamic_slice_in_dim(doc_row, start_row, block_rows, 0)
    query_pos = start_row + jnp.arange(block_rows, dtype=jnp.int32)
    key_pos = jnp.arange(length, dtype=jnp.int32)
    return (doc_block[:, None] == doc_row[None, :]) & (key_pos[None, :] <= query_pos[:, None])


def group_heads(matrix, group_index):
    group_width = HG * HD
    return matrix[:, group_index * group_width : (group_index + 1) * group_width].reshape(
        matrix.shape[0], HG, HD
    )


def attend_row(query_row, key_row, value_row, doc_row):
    length = query_row.shape[0]
    block_rows = min(512, length)

    def one_block(block_index):
        start_row = block_index * block_rows
        visible = block_visible(doc_row, start_row, block_rows)
        query_block = lax.dynamic_slice_in_dim(query_row, start_row, block_rows, 0)
        outputs = []
        logsums = []
        for group_index in range(G):
            scores = (
                jnp.einsum(
                    "qhd,khd->hqk",
                    group_heads(query_block, group_index),
                    group_heads(key_row, group_index),
                    preferred_element_type=jnp.float32,
                )
                * SCORE_SCALE
            )
            scores = jnp.where(visible[None], scores, NEGATIVE)
            largest = jnp.max(scores, axis=-1, keepdims=True)
            powers = jnp.exp(scores - largest)
            totals = jnp.sum(powers, axis=-1, keepdims=True)
            weights = (powers / totals).astype(jnp.bfloat16)
            mixed_heads = jnp.einsum(
                "hqk,khd->qhd",
                weights,
                group_heads(value_row, group_index),
                preferred_element_type=jnp.float32,
            )
            outputs.append(mixed_heads.reshape(block_rows, HG * HD))
            logsums.append(largest[:, :, 0] + jnp.log(totals[:, :, 0]))
        return (jnp.concatenate(outputs, axis=1), jnp.concatenate(logsums, axis=0))

    attended, logsums = lax.map(one_block, jnp.arange(length // block_rows, dtype=jnp.int32))
    return (attended.reshape(length, -1), logsums)


def attend_row_back(query_row, key_row, value_row, doc_row, logsums, grad_row):
    length = query_row.shape[0]
    block_rows = min(512, length)
    row_width = query_row.shape[1]

    def one_block(carry, block_items):
        grad_keys, grad_values = carry
        block_index, block_logsums = block_items
        start_row = block_index * block_rows
        visible = block_visible(doc_row, start_row, block_rows)
        query_block = lax.dynamic_slice_in_dim(query_row, start_row, block_rows, 0)
        grad_block = lax.dynamic_slice_in_dim(grad_row, start_row, block_rows, 0)
        query_parts = []
        key_parts = []
        value_parts = []
        for group_index in range(G):
            query_heads = group_heads(query_block, group_index)
            key_heads = group_heads(key_row, group_index)
            value_heads = group_heads(value_row, group_index)
            grad_heads = group_heads(grad_block, group_index)
            scores = (
                jnp.einsum(
                    "qhd,khd->hqk", query_heads, key_heads, preferred_element_type=jnp.float32
                )
                * SCORE_SCALE
            )
            group_logsums = block_logsums[group_index * HG : (group_index + 1) * HG]
            probs = jnp.where(visible[None], jnp.exp(scores - group_logsums[:, :, None]), 0.0)
            grad_probs = jnp.einsum(
                "qhd,khd->hqk", grad_heads, value_heads, preferred_element_type=jnp.float32
            )
            value_term = jnp.einsum(
                "hqk,qhd->khd",
                probs.astype(jnp.bfloat16),
                grad_heads,
                preferred_element_type=jnp.float32,
            )
            value_parts.append(value_term.reshape(length, HG * HD))
            inner_sums = jnp.sum(probs * grad_probs, axis=-1, keepdims=True)
            grad_scores = (probs * (grad_probs - inner_sums)).astype(jnp.bfloat16)
            query_term = (
                jnp.einsum(
                    "hqk,khd->qhd", grad_scores, key_heads, preferred_element_type=jnp.float32
                )
                * SCORE_SCALE
            )
            key_term = (
                jnp.einsum(
                    "hqk,qhd->khd", grad_scores, query_heads, preferred_element_type=jnp.float32
                )
                * SCORE_SCALE
            )
            query_parts.append(query_term.reshape(block_rows, HG * HD))
            key_parts.append(key_term.reshape(length, HG * HD))
        grad_keys = grad_keys + jnp.concatenate(key_parts, axis=1)
        grad_values = grad_values + jnp.concatenate(value_parts, axis=1)
        return ((grad_keys, grad_values), jnp.concatenate(query_parts, axis=1))

    zero_grads = jnp.zeros((length, row_width), jnp.float32)
    block_ids = jnp.arange(length // block_rows, dtype=jnp.int32)
    (grad_keys, grad_values), grad_queries = lax.scan(
        one_block, (zero_grads, zero_grads), (block_ids, logsums)
    )
    return (grad_queries.reshape(length, row_width), grad_keys, grad_values)


def forward_row(row_items):
    return attend_row(row_items[0], row_items[1], row_items[2], row_items[3])


def backward_row(row_items):
    return attend_row_back(
        row_items[0], row_items[1], row_items[2], row_items[3], row_items[4], row_items[5]
    )


def split_lead(grads, pieces):
    return tuple(
        (grad.reshape((pieces, grad.shape[0] // pieces) + grad.shape[1:]) for grad in grads)
    )


def shards(
    tokens,
    doc_ids,
    norm_in,
    query_weight,
    latent_weight,
    key_up_weight,
    value_up_weight,
    output_weight,
    norm_mid,
    gate_weight,
    up_weight,
    down_weight,
    cotangent,
):
    gathered = (
        lax.all_gather(norm_in, ("dp", "fsdp"), axis=0, tiled=True),
        lax.all_gather(query_weight, ("dp", "fsdp"), axis=0, tiled=True),
        lax.all_gather(latent_weight, ("dp", "fsdp"), axis=0, tiled=True),
        lax.all_gather(key_up_weight, ("dp", "fsdp"), axis=0, tiled=True),
        lax.all_gather(value_up_weight, ("dp", "fsdp"), axis=0, tiled=True),
        lax.all_gather(output_weight, ("dp", "fsdp"), axis=0, tiled=True),
        lax.all_gather(norm_mid, ("dp", "fsdp"), axis=0, tiled=True),
        lax.all_gather(gate_weight, ("dp", "fsdp"), axis=0, tiled=True),
        lax.all_gather(up_weight, ("dp", "fsdp"), axis=0, tiled=True),
        lax.all_gather(down_weight, ("dp", "fsdp"), axis=0, tiled=True),
    )
    (
        gain_in,
        query_mat,
        latent_mat,
        key_mat,
        value_mat,
        output_mat,
        gain_mid,
        gate_mat,
        up_mat,
        down_mat,
    ) = gathered
    rows_here, length = doc_ids.shape
    token_count = tokens.shape[0]
    inputs = tokens.astype(jnp.float32)
    normed_in, unit_in, root_in = rms_parts(inputs, gain_in.astype(jnp.float32))
    normed_low = normed_in.astype(jnp.bfloat16)
    queries = jnp.dot(normed_low, query_mat, preferred_element_type=jnp.float32).astype(
        jnp.bfloat16
    )
    latents = jnp.dot(normed_low, latent_mat, preferred_element_type=jnp.float32).astype(
        jnp.bfloat16
    )
    key_heads = latent_up(latents, key_mat).astype(jnp.bfloat16)
    value_heads = latent_up(latents, value_mat).astype(jnp.bfloat16)
    query_rows = queries.reshape(rows_here, length, -1)
    key_rows = key_heads.reshape(rows_here, length, -1)
    value_rows = value_heads.reshape(rows_here, length, -1)
    attended, logsums = lax.map(forward_row, (query_rows, key_rows, value_rows, doc_ids))
    attended = attended.reshape(token_count, -1).astype(jnp.bfloat16)
    hidden = inputs + jnp.dot(attended, output_mat, preferred_element_type=jnp.float32)
    normed_mid, unit_mid, root_mid = rms_parts(hidden, gain_mid.astype(jnp.float32))
    mid_low = normed_mid.astype(jnp.bfloat16)
    gate_pre = jnp.dot(mid_low, gate_mat, preferred_element_type=jnp.float32)
    up_pre = jnp.dot(mid_low, up_mat, preferred_element_type=jnp.float32)
    sigmoid_gate = jax.nn.sigmoid(gate_pre)
    silu_gate = gate_pre * sigmoid_gate
    activated = (silu_gate * up_pre).astype(jnp.bfloat16)
    layer_out = (hidden + jnp.dot(activated, down_mat, preferred_element_type=jnp.float32)).astype(
        jnp.bfloat16
    )
    held_shards, held_out = lax.optimization_barrier(
        (
            (
                norm_in,
                query_weight,
                latent_weight,
                key_up_weight,
                value_up_weight,
                output_weight,
                norm_mid,
                gate_weight,
                up_weight,
                down_weight,
            ),
            layer_out,
        )
    )
    (
        shard_gain_in,
        shard_query,
        shard_latent,
        shard_key,
        shard_value,
        shard_output,
        shard_gain_mid,
        shard_gate,
        shard_up,
        shard_down,
    ) = held_shards
    regathered = (
        lax.all_gather(shard_gain_in, ("dp", "fsdp"), axis=0, tiled=True),
        lax.all_gather(shard_query, ("dp", "fsdp"), axis=0, tiled=True),
        lax.all_gather(shard_latent, ("dp", "fsdp"), axis=0, tiled=True),
        lax.all_gather(shard_key, ("dp", "fsdp"), axis=0, tiled=True),
        lax.all_gather(shard_value, ("dp", "fsdp"), axis=0, tiled=True),
        lax.all_gather(shard_output, ("dp", "fsdp"), axis=0, tiled=True),
        lax.all_gather(shard_gain_mid, ("dp", "fsdp"), axis=0, tiled=True),
        lax.all_gather(shard_gate, ("dp", "fsdp"), axis=0, tiled=True),
        lax.all_gather(shard_up, ("dp", "fsdp"), axis=0, tiled=True),
        lax.all_gather(shard_down, ("dp", "fsdp"), axis=0, tiled=True),
    )
    (
        gain_in,
        query_mat,
        latent_mat,
        key_mat,
        value_mat,
        output_mat,
        gain_mid,
        gate_mat,
        up_mat,
        down_mat,
    ) = regathered
    layer_out = held_out
    grad_result = cotangent.astype(jnp.float32)
    grad_down = jnp.einsum("nf,nd->fd", activated, cotangent, preferred_element_type=jnp.float32)
    grad_activated = jnp.einsum(
        "nd,fd->nf", cotangent, down_mat, preferred_element_type=jnp.float32
    ).astype(jnp.bfloat16)
    grad_act_wide = grad_activated.astype(jnp.float32)
    grad_gate_pre = (
        grad_act_wide * up_pre * sigmoid_gate * (1.0 + gate_pre * (1.0 - sigmoid_gate))
    ).astype(jnp.bfloat16)
    grad_up_pre = (grad_act_wide * silu_gate).astype(jnp.bfloat16)
    grad_gate = jnp.einsum("nd,nf->df", mid_low, grad_gate_pre, preferred_element_type=jnp.float32)
    grad_up = jnp.einsum("nd,nf->df", mid_low, grad_up_pre, preferred_element_type=jnp.float32)
    grad_mid = jnp.einsum(
        "nf,df->nd", grad_gate_pre, gate_mat, preferred_element_type=jnp.float32
    ) + jnp.einsum("nf,df->nd", grad_up_pre, up_mat, preferred_element_type=jnp.float32)
    grad_hidden_norm, grad_norm_mid = rms_back(
        grad_mid, unit_mid, root_mid, gain_mid.astype(jnp.float32)
    )
    grad_hidden = grad_result + grad_hidden_norm
    grad_branch = grad_hidden.astype(jnp.bfloat16)
    grad_output = jnp.einsum("nf,nd->fd", attended, grad_branch, preferred_element_type=jnp.float32)
    grad_attended = jnp.einsum(
        "nd,fd->nf", grad_branch, output_mat, preferred_element_type=jnp.float32
    ).astype(jnp.bfloat16)
    grad_attended_rows = grad_attended.reshape(rows_here, length, -1)
    grad_queries, grad_keys, grad_values = lax.map(
        backward_row, (query_rows, key_rows, value_rows, doc_ids, logsums, grad_attended_rows)
    )
    grad_queries = grad_queries.reshape(token_count, -1).astype(jnp.bfloat16)
    grad_keys = grad_keys.reshape(token_count, -1).astype(jnp.bfloat16)
    grad_values = grad_values.reshape(token_count, -1).astype(jnp.bfloat16)
    grad_key_up, latent_from_keys = latent_back(latents, key_mat, grad_keys)
    grad_value_up, latent_from_values = latent_back(latents, value_mat, grad_values)
    grad_latents = (latent_from_keys + latent_from_values).astype(jnp.bfloat16)
    grad_query = jnp.einsum(
        "nd,nf->df", normed_low, grad_queries, preferred_element_type=jnp.float32
    )
    grad_latent = jnp.einsum(
        "nd,nf->df", normed_low, grad_latents, preferred_element_type=jnp.float32
    )
    grad_in = jnp.einsum(
        "nf,df->nd", grad_queries, query_mat, preferred_element_type=jnp.float32
    ) + jnp.einsum("nf,df->nd", grad_latents, latent_mat, preferred_element_type=jnp.float32)
    grad_input_norm, grad_norm_in = rms_back(grad_in, unit_in, root_in, gain_in.astype(jnp.float32))
    grad_tokens = (grad_hidden + grad_input_norm).astype(jnp.bfloat16)
    all_grads = (
        grad_norm_in,
        grad_query,
        grad_latent,
        grad_key_up,
        grad_value_up,
        grad_output,
        grad_norm_mid,
        grad_gate,
        grad_up,
        grad_down,
    )
    outer_count = lax.axis_size("dp")
    inner_count = lax.axis_size("fsdp")
    slabs = split_lead(all_grads, outer_count)
    g0, g1, g2, g3, g4, g5, g6, g7, g8, g9 = slabs
    received = (
        lax.all_to_all(
            g0.astype(jnp.bfloat16), "dp", split_axis=0, concat_axis=0, tiled=True
        ).astype(g0.dtype),
        lax.all_to_all(
            g1.astype(jnp.bfloat16), "dp", split_axis=0, concat_axis=0, tiled=True
        ).astype(g1.dtype),
        lax.all_to_all(
            g2.astype(jnp.bfloat16), "dp", split_axis=0, concat_axis=0, tiled=True
        ).astype(g2.dtype),
        lax.all_to_all(
            g3.astype(jnp.bfloat16), "dp", split_axis=0, concat_axis=0, tiled=True
        ).astype(g3.dtype),
        lax.all_to_all(
            g4.astype(jnp.bfloat16), "dp", split_axis=0, concat_axis=0, tiled=True
        ).astype(g4.dtype),
        lax.all_to_all(
            g5.astype(jnp.bfloat16), "dp", split_axis=0, concat_axis=0, tiled=True
        ).astype(g5.dtype),
        lax.all_to_all(
            g6.astype(jnp.bfloat16), "dp", split_axis=0, concat_axis=0, tiled=True
        ).astype(g6.dtype),
        lax.all_to_all(
            g7.astype(jnp.bfloat16), "dp", split_axis=0, concat_axis=0, tiled=True
        ).astype(g7.dtype),
        lax.all_to_all(
            g8.astype(jnp.bfloat16), "dp", split_axis=0, concat_axis=0, tiled=True
        ).astype(g8.dtype),
        lax.all_to_all(
            g9.astype(jnp.bfloat16), "dp", split_axis=0, concat_axis=0, tiled=True
        ).astype(g9.dtype),
    )
    outer_sums = tuple((jnp.sum(piece, axis=0) for piece in received))
    h0, h1, h2, h3, h4, h5, h6, h7, h8, h9 = split_lead(outer_sums, inner_count)
    second = (
        lax.all_to_all(
            h0.astype(jnp.bfloat16), "fsdp", split_axis=0, concat_axis=0, tiled=True
        ).astype(h0.dtype),
        lax.all_to_all(
            h1.astype(jnp.bfloat16), "fsdp", split_axis=0, concat_axis=0, tiled=True
        ).astype(h1.dtype),
        lax.all_to_all(
            h2.astype(jnp.bfloat16), "fsdp", split_axis=0, concat_axis=0, tiled=True
        ).astype(h2.dtype),
        lax.all_to_all(
            h3.astype(jnp.bfloat16), "fsdp", split_axis=0, concat_axis=0, tiled=True
        ).astype(h3.dtype),
        lax.all_to_all(
            h4.astype(jnp.bfloat16), "fsdp", split_axis=0, concat_axis=0, tiled=True
        ).astype(h4.dtype),
        lax.all_to_all(
            h5.astype(jnp.bfloat16), "fsdp", split_axis=0, concat_axis=0, tiled=True
        ).astype(h5.dtype),
        lax.all_to_all(
            h6.astype(jnp.bfloat16), "fsdp", split_axis=0, concat_axis=0, tiled=True
        ).astype(h6.dtype),
        lax.all_to_all(
            h7.astype(jnp.bfloat16), "fsdp", split_axis=0, concat_axis=0, tiled=True
        ).astype(h7.dtype),
        lax.all_to_all(
            h8.astype(jnp.bfloat16), "fsdp", split_axis=0, concat_axis=0, tiled=True
        ).astype(h8.dtype),
        lax.all_to_all(
            h9.astype(jnp.bfloat16), "fsdp", split_axis=0, concat_axis=0, tiled=True
        ).astype(h9.dtype),
    )
    owned = tuple((jnp.sum(piece, axis=0) for piece in second))
    return (layer_out, grad_tokens) + tuple(owned)


def solution(mesh):
    placed = (
        P(("dp", "fsdp"), None),
        P(("dp", "fsdp"), None),
        P(("dp", "fsdp")),
        P(("dp", "fsdp"), None),
        P(("dp", "fsdp"), None),
        P(("dp", "fsdp"), None),
        P(("dp", "fsdp"), None),
        P(("dp", "fsdp"), None),
        P(("dp", "fsdp")),
        P(("dp", "fsdp"), None),
        P(("dp", "fsdp"), None),
        P(("dp", "fsdp"), None),
        P(("dp", "fsdp"), None),
    )
    return jax.shard_map(
        shards,
        mesh=mesh,
        in_specs=placed,
        out_specs=(
            P(("dp", "fsdp"), None),
            P(("dp", "fsdp"), None),
            P(("dp", "fsdp")),
            P(("dp", "fsdp"), None),
            P(("dp", "fsdp"), None),
            P(("dp", "fsdp"), None),
            P(("dp", "fsdp"), None),
            P(("dp", "fsdp"), None),
            P(("dp", "fsdp")),
            P(("dp", "fsdp"), None),
            P(("dp", "fsdp"), None),
            P(("dp", "fsdp"), None),
        ),
        check_vma=False,
    )
```

profile of v0, /device:TPU:0, one launch (start us, length us, event | category | flops | bytes accessed | tf_op | source)
XLA Modules:
  0.0 1448.7 jit_solution(4167313827356066115)
XLA Ops:
  12.9 42.0 %all-reduce.5 = (bf16[1024]{0:T(1024)(128)(2,1)S(1)}, bf16[1024]{0:T(1024)(128)(2,1)S(1)}) all-reduce(bf16[1024]{0:T(1024)(128)(2,1)S(1)} %dynamic-update-slice, bf16[1024]{0:T(1024)(128)(2,1)S(1)} %dynamic-update-slice.1), channel_id=1, replica_groups=mesh['dp'=4,'fsdp'=8] {'dp','fsdp'}, use_global_device_ids=true, to_apply=%add | all-reduce | flops 2048 | bytes 8192
  55.5 69.6 %all_gather.63 = bf16[512,512]{1,0:T(8,128)(2,1)S(1)} all-gather(bf16[16,512]{1,0:T(8,128)(2,1)} %param.22), channel_id=1, replica_groups=mesh['dp'=4,'fsdp'=8] {'dp','fsdp'}, dimensions={0}, use_global_device_ids=true | all-gather | bytes 540672 | tf_op jit(solution)/shard_map/all_gather | solution.py:207
  125.1 67.8 %all_gather.64 = bf16[512,512]{1,0:T(8,128)(2,1)S(1)} all-gather(bf16[16,512]{1,0:T(8,128)(2,1)} %param.23), channel_id=1, replica_groups=mesh['dp'=4,'fsdp'=8] {'dp','fsdp'}, dimensions={0}, use_global_device_ids=true | all-gather | bytes 540672 | tf_op jit(solution)/shard_map/all_gather | solution.py:208
  217.1 102.5 %while.47 = (s32[]{:T(128)}, bf16[2,512,1024]{2,1,0:T(8,128)(2,1)}, f32[2,16,512]{2,1,0:T(8,128)}, s32[2]{0:T(128)S(1)}, s32[1024]{0:T(1024)S(1)}, /*index=5*/bf...) while((s32[]{:T(128)}, bf16[2,512,1024]{2,1,0:T(8,128)(2,1)}, ...), condition=%wide.region_6.7_spmd, body=%wide.region_1.6_spmd.sunk | while | flops 2251817472 | bytes 177551664 | solution.py:102
  231.0 14.9 %fusion.171 = (f32[8,512]{1,0:T(8,128)S(1)}, f32[8,512]{1,0:T(8,128)S(1)}, f32[8,512,1024]{2,1,0:T(8,128)}) fusion(f32[8,512,1024]{2,1,0:T(8,128)} %get-tuple-element.570, f32[8,512]{1,0:T(8,128)S(1)} %get-tuple-element.571, pred[512,1024]{1,0:T(8,128)(4,1)S(1)} %fusion.169, bf16[512,8,64]{0,2,1:T(8,128)(2,1)S(1)} %bitcast.310, ...), kind=kOutput, calls=%fused_computation.8.clone.1 | convolution fusion | flops 566222848 | bytes 35700736 | tf_op jit(solution)/shard_map/while/body/eval_jaxpr/while/body/eval_jaxpr/qhd,khd->hqk/dot_general | solution.py:79
  282.1 14.2 fusion.171
  340.1 15.7 %multiply_convert_fusion.2 = (bf16[1024,2816]{1,0:T(8,128)(2,1)}, f32[1024,2816]{1,0:T(8,128)}) fusion(f32[1024,2816]{1,0:T(8,128)} %fusion.47, bf16[1024,1024]{0,1:T(8,128)(2,1)S(1)} %multiply_convert_fusion.3, bf16[1024,2816]{1,0:T(8,128)(2,1)} %all-gather.21.cloned.1.call-done), kind=kOutput, calls=%fused_computation.57 | convolution fusion | flops 5922881536 | bytes 36700160 | tf_op jit(solution)/shard_map/dot_general | solution.py:249
  355.8 37.5 %all-gather.23.cloned.1.call-done = bf16[2816,1024]{1,0:T(8,128)(2,1)} async-done(((bf16[88,1024]{1,0:T(8,128)(2,1)}), bf16[2816,1024]{1,0:T(8,128)(2,1)}) %all-gather.23.cloned.1.call-update) | async-done | bytes 5767184 | tf_op jit(solution)/shard_map/all_gather | solution.py:213
  427.3 108.8 %all-reduce.4 = (bf16[1024]{0:T(1024)(128)(2,1)S(1)}, bf16[1024]{0:T(1024)(128)(2,1)S(1)}) all-reduce(bf16[1024]{0:T(1024)(128)(2,1)S(1)} %dynamic-update-slice.2, bf16[1024]{0:T(1024)(128)(2,1)S(1)} %dynamic-update-slice.3), channel_id=1, replica_groups=mesh['dp'=4,'fsdp'=8] {'dp','fsdp'}, use_global_device_ids=true, to_apply=%add.2 | all-reduce | flops 2048 | bytes 8192
  536.7 75.0 %all_gather.76 = bf16[512,512]{1,0:T(8,128)(2,1)} all-gather(bf16[16,512]{1,0:T(8,128)(2,1)S(1)} %copy-done.38), channel_id=1, replica_groups=mesh['dp'=4,'fsdp'=8] {'dp','fsdp'}, dimensions={0}, use_global_device_ids=true | all-gather | bytes 540672 | tf_op jit(solution)/shard_map/all_gather | solution.py:289
  611.7 72.8 %all_gather.77 = bf16[512,512]{1,0:T(8,128)(2,1)} all-gather(bf16[16,512]{1,0:T(8,128)(2,1)S(1)} %copy-done.39), channel_id=1, replica_groups=mesh['dp'=4,'fsdp'=8] {'dp','fsdp'}, dimensions={0}, use_global_device_ids=true | all-gather | bytes 540672 | tf_op jit(solution)/shard_map/all_gather | solution.py:290
  694.9 20.0 %fusion.20 = (bf16[1024,2816]{1,0:T(8,128)(2,1)}, bf16[1024,2816]{1,0:T(8,128)(2,1)}) fusion(f32[1024,2816]{1,0:T(8,128)} %fusion.47, f32[1024,2816]{1,0:T(8,128)} %get-tuple-element.432, bf16[2816,1024]{1,0:T(8,128)(2,1)} %all-gather.25.cloned.1.call-done, bf16[1024,1024]{1,0:T(8,128)(2,1)} %param.29), kind=kOutput, calls=%fused_computation.56 | convolution fusion | flops 5948833792 | bytes 42467328 | tf_op jit(solution)/shard_map/nd,fd->nf/dot_general | solution.py:312
  726.1 12.9 multiply_reduce_fusion.2
  750.2 241.9 %while.48 = (s32[]{:T(128)}, f32[1024,1024]{0,1:T(8,128)}, f32[1024,1024]{0,1:T(8,128)}, bf16[2,512,1024]{2,1,0:T(8,128)(2,1)}, s32[2]{0:T(128)S(1)}, /*index=5*...) while((s32[]{:T(128)}, f32[1024,1024]{0,1:T(8,128)}, ...), condition=%wide.region_12.13_spmd.clone, body=%wide.region_9.12_spmd.clone.sunk | while | flops 5456257536 | bytes 392870432 | solution.py:166
  773.7 13.6 multiply_reduce_fusion.7
  787.4 15.1 %multiply_convert_fusion.6 = bf16[8,512,1024]{2,1,0:T(8,128)(2,1)} fusion(f32[8,512,1024]{2,1,0:T(8,128)} %get-tuple-element.594, f32[8,512,1024]{2,1,0:T(8,128)} %fusion.197, f32[8,512]{1,0:T(8,128)} %get-tuple-element.595), kind=kLoop, calls=%fused_computation.26.clone.1 | loop fusion | flops 12582912 | bytes 41959424 | tf_op jit(solution)/shard_map/while/body/eval_jaxpr/while/body/eval_jaxpr/convert_element_type | solution.py:145
  893.4 13.7 multiply_reduce_fusion.7
  907.1 14.9 %multiply_convert_fusion.6 = bf16[8,512,1024]{2,1,0:T(8,128)(2,1)} fusion(f32[8,512,1024]{2,1,0:T(8,128)} %get-tuple-element.594, f32[8,512,1024]{2,1,0:T(8,128)} %fusion.197, f32[8,512]{1,0:T(8,128)} %get-tuple-element.595), kind=kLoop, calls=%fused_computation.26.clone.1 | loop fusion | flops 12582912 | bytes 41959424 | tf_op jit(solution)/shard_map/while/body/eval_jaxpr/while/body/eval_jaxpr/convert_element_type | solution.py:145
  1089.6 12.6 all-to-all-done.4
  1135.4 19.9 %all-to-all-done.10 = bf16[4,256,1024]{2,1,0:T(8,128)(2,1)} async-done(((bf16[4,256,1024]{2,1,0:T(8,128)(2,1)}), bf16[4,256,1024]{2,1,0:T(8,128)(2,1)}, u32[]{:S(2)}, u32[]{:S(2)}) %all-to-all-start.10) | async-done | bytes 2097184 | tf_op jit(solution)/shard_map/all_to_all | solution.py:387
  1162.7 22.8 %all-to-all-done.2 = bf16[4,256,1024]{2,1,0:T(8,128)(2,1)} async-done(((bf16[4,256,1024]{2,1,0:T(8,128)(2,1)}), bf16[4,256,1024]{2,1,0:T(8,128)(2,1)}, u32[]{:S(2)}, u32[]{:S(2)}) %all-to-all-start.2) | async-done | bytes 2097184 | tf_op jit(solution)/shard_map/all_to_all | solution.py:375
  1238.8 54.2 %all-to-all-done.16 = bf16[4,256,2816]{2,1,0:T(8,128)(2,1)} async-done(((bf16[4,256,2816]{2,1,0:T(8,128)(2,1)}), bf16[4,256,2816]{2,1,0:T(8,128)(2,1)}, u32[]{:S(2)}, u32[]{:S(2)}) %all-to-all-start.16) | async-done | bytes 5767200 | tf_op jit(solution)/shard_map/all_to_all | solution.py:396
  1303.1 60.1 %all-to-all-done.14 = bf16[4,256,2816]{2,1,0:T(8,128)(2,1)} async-done(((bf16[4,256,2816]{2,1,0:T(8,128)(2,1)}), bf16[4,256,2816]{2,1,0:T(8,128)(2,1)}, u32[]{:S(2)}, u32[]{:S(2)}) %all-to-all-start.14) | async-done | bytes 5767200 | tf_op jit(solution)/shard_map/all_to_all | solution.py:393
  1371.9 29.2 %all-to-all-done.17 = bf16[8,32,2816]{2,1,0:T(8,128)(2,1)S(1)} async-done(((bf16[8,32,2816]{2,1,0:T(8,128)(2,1)}), bf16[8,32,2816]{2,1,0:T(8,128)(2,1)S(1)}, u32[]{:S(2)}, u32[]{:S(2)}) %all-to-all-start.17) | async-done | bytes 1441824 | tf_op jit(solution)/shard_map/all_to_all | solution.py:430
  (369 shorter events, 622.1 us)
Async XLA Ops:
  7.2 191.6 %all-gather.15.cloned.1.call-start = ((), (), s32[]{:S(2)}) async-start(), calls=%async_computation.21 | async-start | bytes 1081344 | tf_op jit(solution)/shard_map/all_gather | solution.py:206
  7.9 198.4 %all-gather.13.cloned.1.call-start = ((), (), s32[]{:S(2)}) async-start(), calls=%async_computation.20 | async-start | bytes 2162688 | tf_op jit(solution)/shard_map/all_gather | solution.py:205
  8.7 311.0 %all-gather.17.cloned.1.call-start = ((), (), s32[]{:S(2)}) async-start(), calls=%async_computation.22 | async-start | bytes 2162688 | tf_op jit(solution)/shard_map/all_gather | solution.py:209
  9.4 318.4 %all-gather.19.cloned.1.call-start = ((), (), s32[]{:S(2)}) async-start(), calls=%async_computation.23 | async-start | bytes 5947392 | tf_op jit(solution)/shard_map/all_gather | solution.py:211
  10.0 330.1 %all-gather.21.cloned.1.call-start = ((), (), s32[]{:S(2)}) async-start(), calls=%async_computation.24 | async-start | bytes 5947392 | tf_op jit(solution)/shard_map/all_gather | solution.py:212
  10.6 382.7 %all-gather.23.cloned.1.call-start = ((), (), s32[]{:S(2)}) async-start(), calls=%async_computation.25 | async-start | bytes 5947392 | tf_op jit(solution)/shard_map/all_gather | solution.py:213
  11.1 683.8 %all-gather.25.cloned.1.call-start = ((), (), s32[]{:S(2)}) async-start(), calls=%async_computation.26 | async-start | bytes 5947392 | tf_op jit(solution)/shard_map/all_gather | solution.py:295
  405.1 309.8 %all-gather.27.cloned.1.call-start = ((), (), s32[]{:S(2)}) async-start(), calls=%async_computation.27 | async-start | bytes 5947392 | tf_op jit(solution)/shard_map/all_gather | solution.py:293
  405.9 320.3 %all-gather.29.cloned.1.call-start = ((), (), s32[]{:S(2)}) async-start(), calls=%async_computation.28 | async-start | bytes 5947392 | tf_op jit(solution)/shard_map/all_gather | solution.py:294
  406.6 335.4 %all-gather.31.cloned.1.call-start = ((), (), s32[]{:S(2)}) async-start(), calls=%async_computation.29 | async-start | bytes 2162688 | tf_op jit(solution)/shard_map/all_gather | solution.py:291
  407.2 593.5 %all-gather.33.cloned.1.call-start = ((), (), s32[]{:S(2)}) async-start(), calls=%async_computation.30 | async-start | bytes 2162688 | tf_op jit(solution)/shard_map/all_gather | solution.py:287
  418.6 265.9 %all-to-all-start.18 = ((bf16[4,704,1024]{2,1,0:T(8,128)(2,1)}), bf16[4,704,1024]{2,1,0:T(8,128)(2,1)}, u32[]{:S(2)}, u32[]{:S(2)}) async-start(bf16[4,704,1024]{2,1,0:T(8,128)(2,1)} %bitcast.320), calls=%async_computation.18 | async-start | bytes 11534336 | tf_op jit(solution)/shard_map/all_to_all | solution.py:399
  423.9 586.9 %all-gather.35.cloned.1.call-start = ((), (), s32[]{:S(2)}) async-start(), calls=%async_computation.31 | async-start | bytes 1081344 | tf_op jit(solution)/shard_map/all_gather | solution.py:288
  690.1 317.3 %all-to-all-start.19 = ((bf16[8,88,1024]{2,1,0:T(8,128)(2,1)}), bf16[8,88,1024]{2,1,0:T(8,128)(2,1)}, u32[]{:S(2)}, u32[]{:S(2)}) async-start(bf16[8,88,1024]{2,1,0:T(8,128)(2,1)} %bitcast.53), calls=%async_computation.19 | async-start | bytes 2883584 | tf_op jit(solution)/shard_map/all_to_all | solution.py:433
  1047.6 13.1 all-to-all-start.6
  1084.2 18.0 %all-to-all-start.4 = ((bf16[4,256,512]{2,1,0:T(8,128)(2,1)}), bf16[4,256,512]{2,1,0:T(8,128)(2,1)S(1)}, u32[]{:S(2)}, u32[]{:S(2)}) async-start(bf16[4,256,512]{2,1,0:T(8,128)(2,1)} %convolution_convert_fusion.9), calls=%async_computation.4 | async-start | bytes 2097152 | tf_op jit(solution)/shard_map/all_to_all | solution.py:378
  1124.9 30.4 %all-to-all-start.10 = ((bf16[4,256,1024]{2,1,0:T(8,128)(2,1)}), bf16[4,256,1024]{2,1,0:T(8,128)(2,1)}, u32[]{:S(2)}, u32[]{:S(2)}) async-start(bf16[4,256,1024]{2,1,0:T(8,128)(2,1)} %fusion.36), calls=%async_computation.10 | async-start | bytes 4194304 | tf_op jit(solution)/shard_map/all_to_all | solution.py:387
  1155.3 30.2 %all-to-all-start.2 = ((bf16[4,256,1024]{2,1,0:T(8,128)(2,1)}), bf16[4,256,1024]{2,1,0:T(8,128)(2,1)}, u32[]{:S(2)}, u32[]{:S(2)}) async-start(bf16[4,256,1024]{2,1,0:T(8,128)(2,1)} %convolution_convert_fusion.6), calls=%async_computation.2 | async-start | bytes 4194304 | tf_op jit(solution)/shard_map/all_to_all | solution.py:375
  1185.5 18.3 %all-to-all-start.11 = ((bf16[8,32,1024]{2,1,0:T(8,128)(2,1)}), bf16[8,32,1024]{2,1,0:T(8,128)(2,1)S(1)}, u32[]{:S(2)}, u32[]{:S(2)}) async-start(bf16[8,32,1024]{2,1,0:T(8,128)(2,1)} %bitcast.47), calls=%async_computation.11 | async-start | bytes 1048576 | tf_op jit(solution)/shard_map/all_to_all | solution.py:421
  1203.8 18.2 %all-to-all-start.3 = ((bf16[8,32,1024]{2,1,0:T(8,128)(2,1)}), bf16[8,32,1024]{2,1,0:T(8,128)(2,1)S(1)}, u32[]{:S(2)}, u32[]{:S(2)}) async-start(bf16[8,32,1024]{2,1,0:T(8,128)(2,1)} %bitcast.337), calls=%async_computation.3 | async-start | bytes 1048576 | tf_op jit(solution)/shard_map/all_to_all | solution.py:409
  1222.8 70.2 %all-to-all-start.16 = ((bf16[4,256,2816]{2,1,0:T(8,128)(2,1)}), bf16[4,256,2816]{2,1,0:T(8,128)(2,1)}, u32[]{:S(2)}, u32[]{:S(2)}) async-start(bf16[4,256,2816]{2,1,0:T(8,128)(2,1)} %bitcast.321), calls=%async_computation.16 | async-start | bytes 11534336 | tf_op jit(solution)/shard_map/all_to_all | solution.py:396
  1293.0 70.3 %all-to-all-start.14 = ((bf16[4,256,2816]{2,1,0:T(8,128)(2,1)}), bf16[4,256,2816]{2,1,0:T(8,128)(2,1)}, u32[]{:S(2)}, u32[]{:S(2)}) async-start(bf16[4,256,2816]{2,1,0:T(8,128)(2,1)} %bitcast.322), calls=%async_computation.14 | async-start | bytes 11534336 | tf_op jit(solution)/shard_map/all_to_all | solution.py:393
  1363.2 37.8 %all-to-all-start.17 = ((bf16[8,32,2816]{2,1,0:T(8,128)(2,1)}), bf16[8,32,2816]{2,1,0:T(8,128)(2,1)S(1)}, u32[]{:S(2)}, u32[]{:S(2)}) async-start(bf16[8,32,2816]{2,1,0:T(8,128)(2,1)} %bitcast.51), calls=%async_computation.17 | async-start | bytes 2883584 | tf_op jit(solution)/shard_map/all_to_all | solution.py:430
  1401.0 38.3 %all-to-all-start.15 = ((bf16[8,32,2816]{2,1,0:T(8,128)(2,1)}), bf16[8,32,2816]{2,1,0:T(8,128)(2,1)}, u32[]{:S(2)}, u32[]{:S(2)}) async-start(bf16[8,32,2816]{2,1,0:T(8,128)(2,1)} %bitcast.49), calls=%async_computation.15 | async-start | bytes 2883584 | tf_op jit(solution)/shard_map/all_to_all | solution.py:427
  (72 other events, 1085.3 us)
Sparse Core Ops, SparseCore 0:
  11.0 56.6 all-gather.14
  70.7 55.8 all-gather.12
  129.6 56.8 all-gather.16
  189.3 66.5 all-gather.18
  258.6 65.6 all-gather.20
  327.0 66.1 all-gather.22
  405.2 77.8 all-gather.24
  486.0 69.5 all-gather.26
  558.5 69.0 all-gather.28
  630.4 56.5 all-gather.30
  690.0 61.7 all-gather.32
  754.6 52.6 all-gather.34
where the time goes:
time: 1460 us; the launch traced here: 1450 us
  blocking collectives  436 us (30%)
  matrix products  395 us (27%)
  waiting for transfers between devices  302 us (21%)
  other arithmetic  133 us (9%)
  starting transfers between devices  82.6 us (6%)
  local copies, waits for them, and re-layouts  81.4 us (6%)
  between operations  15 us (1%)
    unnamed x2, blocking collectives  151 us
    all_gather x1, blocking collectives, shards(): lax.all_gather(shard_key, ('dp', 'fsdp'), axis=0, tiled=True)  75 us
    all_gather x1, blocking collectives, shards(): lax.all_gather(shard_value, ('dp', 'fsdp'), axis=0, tiled=True)  72.8 us
    all_gather x1, blocking collectives, shards(): lax.all_gather(key_up_weight, ('dp', 'fsdp'), axis=0, tiled=True)  69.6 us
    all_gather x1, blocking collectives, shards(): lax.all_gather(value_up_weight, ('dp', 'fsdp'), axis=0, tiled=True)  67.8 us
    all_to_all x1, waiting for transfers between devices, shards(): lax.all_to_all(g7.astype(jnp.bfloat16), 'dp', split_axis=0, concat_axis=0...  60.1 us
    all_to_all x1, waiting for transfers between devices, shards(): lax.all_to_all(g8.astype(jnp.bfloat16), 'dp', split_axis=0, concat_axis=0...  54.2 us
    dot_general x4, matrix products, one_block(): jnp.einsum('qhd,khd->hqk', query_heads, key_heads, preferred_element_type...  49.6 us
  transfers between devices with their start and end apart: 32, of which 18 were waited for; matrix products, arithmetic and copies ran while one was open for 40% of the time, Pallas kernels for 0%

commit v1 on v0

v1 whole, which is shorter than its diff:
```python
import functools

import jax
import jax.numpy as jnp
from jax import lax
from jax.experimental import pallas as pl
from jax.experimental.pallas import tpu as pltpu
from jax.sharding import PartitionSpec as P

HD = 64
G = 2
HG = 8
PAIR = 128
EPSILON = 1e-05
SCORE_SCALE = 0.125
NEGATIVE = -1e30
LOG2E = 1.4426950408889634
F32 = jnp.float32
BF16 = jnp.bfloat16
TILE = 256
VMEM_LIMIT = 60 * 1024 * 1024


def nn(a, b):
    return lax.dot_general(a, b, (((1,), (0,)), ((), ())), preferred_element_type=F32)


def nt(a, b):
    return lax.dot_general(a, b, (((1,), (1,)), ((), ())), preferred_element_type=F32)


def tn(a, b):
    return lax.dot_general(a, b, (((0,), (0,)), ((), ())), preferred_element_type=F32)


def params(**extra):
    return pltpu.CompilerParams(vmem_limit_bytes=VMEM_LIMIT, **extra)


def whole(shape):
    return pl.BlockSpec(shape, lambda *_: (0,) * len(shape))


def rows_of(tile, width):
    return pl.BlockSpec((tile, width), lambda i: (i, 0))


def shape_of(shape, dtype):
    return jax.ShapeDtypeStruct(shape, dtype)


def project_kernel(
    tok_ref, wq_ref, wl_ref, wg_ref, ku_ref, vu_ref, q_ref, lat_ref, k_ref, v_ref, n_ref, gain_ref
):
    @pl.when(pl.program_id(0) == 0)
    def _():
        gain_ref[...] = wg_ref[...].astype(F32).T[0:8, :]

    x = tok_ref[...].astype(F32)
    root = lax.rsqrt(jnp.mean(x * x, axis=-1, keepdims=True) + EPSILON)
    normed = (x * root * gain_ref[0:1, :]).astype(BF16)
    n_ref[...] = normed
    q_ref[...] = (nn(normed, wq_ref[...]).astype(BF16).astype(F32) * SCORE_SCALE).astype(BF16)
    lat = nn(normed, wl_ref[...]).astype(BF16)
    lat_ref[...] = lat
    wide = lat.shape[1] // G
    out = k_ref.shape[1] // G
    for g in range(G):
        piece = lat[:, g * wide : (g + 1) * wide]
        k_ref[:, g * out : (g + 1) * out] = nn(
            piece, ku_ref[g * wide : (g + 1) * wide, :]
        ).astype(BF16)
        v_ref[:, g * out : (g + 1) * out] = nn(
            piece, vu_ref[g * wide : (g + 1) * wide, :]
        ).astype(BF16)


def project(tokens, first, ku, vu):
    count, d = tokens.shape
    latw = ku.shape[0]
    width = G * ku.shape[1]
    return pl.pallas_call(
        project_kernel,
        grid=(count // TILE,),
        in_specs=[
            rows_of(TILE, d),
            pl.BlockSpec((d, width), lambda i: (0, 0)),
            pl.BlockSpec((d, latw), lambda i: (0, width // latw)),
            pl.BlockSpec((d, PAIR), lambda i: (0, (width + 2 * latw) // PAIR)),
            whole(ku.shape),
            whole(vu.shape),
        ],
        out_specs=[
            rows_of(TILE, width),
            rows_of(TILE, latw),
            rows_of(TILE, width),
            rows_of(TILE, width),
            rows_of(TILE, d),
            whole((8, d)),
        ],
        out_shape=[
            shape_of((count, width), BF16),
            shape_of((count, latw), BF16),
            shape_of((count, width), BF16),
            shape_of((count, width), BF16),
            shape_of((count, d), BF16),
            shape_of((8, d), F32),
        ],
        compiler_params=params(),
        name="project",
    )(tokens, first, first, first, ku, vu)


def window_of(doc_ref, block):
    start = block * TILE
    here = doc_ref[start]
    one = (doc_ref[start - 1] == here).astype(jnp.int32) if block >= 1 else 0
    two = (doc_ref[start - TILE - 1] == here).astype(jnp.int32) if block >= 2 else 0
    return one + two


def attend_kernel(doc_ref, q_ref, k_ref, v_ref, col_ref, row_ref, o_ref, lse_ref, bias_ref):
    length = q_ref.shape[0]
    blocks = length // TILE
    lane = lax.broadcasted_iota(jnp.int32, (TILE, PAIR), 1)
    low = lane < HD

    @pl.when(pl.program_id(0) == 0)
    def _():
        for b in range(blocks):
            first = max(0, b - 2)
            width = (b - first + 1) * TILE
            qpos = b * TILE + lax.broadcasted_iota(jnp.int32, (TILE, width), 0)
            kpos = first * TILE + lax.broadcasted_iota(jnp.int32, (TILE, width), 1)
            same = (
                col_ref[b * TILE : (b + 1) * TILE, 0:1]
                == row_ref[0:1, first * TILE : first * TILE + width]
            )
            bias_ref[b, :, 3 * TILE - width :] = jnp.where(
                same & (kpos <= qpos), 0.0, NEGATIVE
            )

    for b in range(blocks):
        q = q_ref[b * TILE : (b + 1) * TILE, :]
        zero = jnp.zeros_like(q)
        heads = (jnp.where(low, q, zero), jnp.where(low, zero, q))
        seen = window_of(doc_ref, b)

        def run(extra, b=b, heads=heads):
            width = (extra + 1) * TILE
            at = (b - extra) * TILE
            k = k_ref[at : at + width, :]
            v = v_ref[at : at + width, :]
            vlow = lax.broadcasted_iota(jnp.int32, v.shape, 1) < HD
            one = jnp.ones_like(v)
            values = (jnp.where(vlow, v, one), jnp.where(vlow, one, v))
            bias = bias_ref[b, :, 3 * TILE - width :]
            outs = []
            sums = []
            for h in range(2):
                s = nt(heads[h], k) * LOG2E + bias
                top = jnp.max(s, axis=-1, keepdims=True)
                p = jnp.exp2(s - top)
                o = nn(p.astype(BF16), values[h])
                total = pltpu.roll(o, HD, 1)
                outs.append(o / total)
                sums.append(top + jnp.log2(total))
            o_ref[b * TILE : (b + 1) * TILE, :] = jnp.where(low, outs[0], outs[1]).astype(BF16)
            both = jnp.where(low, sums[0], sums[1]).T
            lse_ref[0, 0:1, b * TILE : (b + 1) * TILE] = both[0:1, :]
            lse_ref[0, 1:2, b * TILE : (b + 1) * TILE] = both[HD : HD + 1, :]

        for extra in range(min(b, 2) + 1):
            pl.when(seen == extra)(functools.partial(run, extra))


def attend(doc, q, k, v):
    length, width = q.shape
    pairs = width // PAIR
    col = doc.reshape(length, 1)
    row = doc.reshape(1, length)
    return pl.pallas_call(
        attend_kernel,
        grid_spec=pltpu.PrefetchScalarGridSpec(
            num_scalar_prefetch=1,
            grid=(pairs,),
            in_specs=[
                pl.BlockSpec((length, PAIR), lambda i, *_: (0, i)),
                pl.BlockSpec((length, PAIR), lambda i, *_: (0, i)),
                pl.BlockSpec((length, PAIR), lambda i, *_: (0, i)),
                whole((length, 1)),
                whole((1, length)),
            ],
            out_specs=[
                pl.BlockSpec((length, PAIR), lambda i, *_: (0, i)),
                pl.BlockSpec((1, 8, length), lambda i, *_: (i, 0, 0)),
            ],
            scratch_shapes=[pltpu.VMEM((length // TILE, TILE, 3 * TILE), F32)],
        ),
        out_shape=[shape_of((length, width), BF16), shape_of((pairs, 8, length), F32)],
        compiler_params=params(),
        name="attend",
    )(doc.reshape(length), q, k, v, col, row)


def attend_back_kernel(
    doc_ref,
    q_ref,
    k_ref,
    v_ref,
    o_ref,
    do_ref,
    lse_ref,
    col_ref,
    row_ref,
    dq_ref,
    dk_ref,
    dv_ref,
    bias_ref,
    dk_acc,
    dv_acc,
):
    length = q_ref.shape[0]
    blocks = length // TILE
    lane = lax.broadcasted_iota(jnp.int32, (TILE, PAIR), 1)
    low = lane < HD

    @pl.when(pl.program_id(0) == 0)
    def _():
        for b in range(blocks):
            first = max(0, b - 2)
            width = (b - first + 1) * TILE
            kpos = first * TILE + lax.broadcasted_iota(jnp.int32, (width, TILE), 0)
            qpos = b * TILE + lax.broadcasted_iota(jnp.int32, (width, TILE), 1)
            same = (
                col_ref[first * TILE : first * TILE + width, 0:1]
                == row_ref[0:1, b * TILE : (b + 1) * TILE]
            )
            bias_ref[b, 3 * TILE - width :, :] = jnp.where(
                same & (kpos <= qpos), 0.0, NEGATIVE
            )

    dk_acc[...] = jnp.zeros_like(dk_acc)
    dv_acc[...] = jnp.zeros_like(dv_acc)
    for b in range(blocks):
        rows = slice(b * TILE, (b + 1) * TILE)
        q = q_ref[rows, :]
        do = do_ref[rows, :]
        zero = jnp.zeros_like(q)
        prod = (do.astype(F32) * o_ref[rows, :].astype(F32)).T
        inner = (
            jnp.sum(prod[0:HD, :], axis=0, keepdims=True),
            jnp.sum(prod[HD:, :], axis=0, keepdims=True),
        )
        seen = window_of(doc_ref, b)

        def run(extra, b=b, rows=rows, q=q, do=do, zero=zero, inner=inner):
            width = (extra + 1) * TILE
            at = (b - extra) * TILE
            keys = slice(at, at + width)
            k = k_ref[keys, :]
            v = v_ref[keys, :]
            bias = bias_ref[b, 3 * TILE - width :, :]
            parts = []
            dks = []
            dvs = []
            for h in range(2):
                mine = low if h == 0 else ~low
                qh = jnp.where(mine, q, zero)
                doh = jnp.where(mine, do, zero)
                s = nt(k, qh) * LOG2E + bias
                p = jnp.exp2(s - lse_ref[0, h : h + 1, rows])
                dp = nt(v, doh)
                ds = (p * (dp - inner[h])).astype(BF16)
                dvs.append(nn(p.astype(BF16), doh))
                dks.append(nn(ds, qh))
                parts.append(tn(ds, k))
            dv_acc[keys, :] += dvs[0] + dvs[1]
            dk_acc[keys, :] += dks[0] + dks[1]
            dq_ref[rows, :] = (jnp.where(low, parts[0], parts[1]) * SCORE_SCALE).astype(BF16)

        for extra in range(min(b, 2) + 1):
            pl.when(seen == extra)(functools.partial(run, extra))
    dk_ref[...] = dk_acc[...].astype(BF16)
    dv_ref[...] = dv_acc[...].astype(BF16)


def attend_back(doc, q, k, v, o, do, lse):
    length, width = q.shape
    pairs = width // PAIR
    col = doc.reshape(length, 1)
    row = doc.reshape(1, length)
    strip = pl.BlockSpec((length, PAIR), lambda i, *_: (0, i))
    return pl.pallas_call(
        attend_back_kernel,
        grid_spec=pltpu.PrefetchScalarGridSpec(
            num_scalar_prefetch=1,
            grid=(pairs,),
            in_specs=[strip] * 5
            + [
                pl.BlockSpec((1, 8, length), lambda i, *_: (i, 0, 0)),
                whole((length, 1)),
                whole((1, length)),
            ],
            out_specs=[strip] * 3,
            scratch_shapes=[
                pltpu.VMEM((length // TILE, 3 * TILE, TILE), F32),
                pltpu.VMEM((length, PAIR), F32),
                pltpu.VMEM((length, PAIR), F32),
            ],
        ),
        out_shape=[shape_of((length, width), BF16)] * 3,
        compiler_params=params(),
        name="attend_back",
    )(doc.reshape(length), q, k, v, o, do, lse, col, row)


def middle_kernel(att_ref, wo_ref, tok_ref, gain_ref, hid_ref, mid_ref, midt_ref):
    hid = tok_ref[...].astype(F32) + nn(att_ref[...], wo_ref[...])
    hid_ref[...] = hid
    root = lax.rsqrt(jnp.mean(hid * hid, axis=-1, keepdims=True) + EPSILON)
    mid = (hid * root * gain_ref[1:2, :]).astype(BF16)
    mid_ref[...] = mid
    midt_ref[...] = mid.T


def middle(att, wo, tokens, gains):
    count, d = tokens.shape
    width = att.shape[1]
    return pl.pallas_call(
        middle_kernel,
        grid=(count // TILE,),
        in_specs=[rows_of(TILE, width), wo[1], rows_of(TILE, d), whole((8, d))],
        out_specs=[
            rows_of(TILE, d),
            rows_of(TILE, d),
            pl.BlockSpec((d, TILE), lambda i: (0, i)),
        ],
        out_shape=[
            shape_of((count, d), F32),
            shape_of((count, d), BF16),
            shape_of((d, count), BF16),
        ],
        compiler_params=params(),
        name="middle",
    )(att, wo[0], tokens, gains)


def feed_kernel(
    mid_ref,
    midt_ref,
    cot_ref,
    hid_ref,
    gmid_in_ref,
    gate_ref,
    up_ref,
    down_ref,
    out_ref,
    gmid_ref,
    ggate_ref,
    gup_ref,
    gdown_ref,
    act_s,
    ggp_s,
    gup_s,
):
    count = mid_ref.shape[0]

    @pl.when(pl.program_id(0) == 0)
    def _():
        out_ref[...] = hid_ref[...]
        if gmid_in_ref is None:
            gmid_ref[...] = jnp.zeros_like(gmid_ref)
        else:
            gmid_ref[...] = gmid_in_ref[...]

    gate = gate_ref[...]
    up = up_ref[...]
    down = down_ref[...]

    @pl.loop(0, count // TILE)
    def _(t):
        rows = pl.ds(pl.multiple_of(t * TILE, TILE), TILE)
        m = mid_ref[rows, :]
        gate_pre = nn(m, gate)
        up_pre = nn(m, up)
        grad_act = nt(cot_ref[rows, :], down).astype(BF16).astype(F32)
        sig = 1.0 / (1.0 + jnp.exp(-gate_pre))
        silu = gate_pre * sig
        act = (silu * up_pre).astype(BF16)
        ggp = (grad_act * up_pre * (sig * (1.0 + gate_pre * (1.0 - sig)))).astype(BF16)
        gup = (grad_act * silu).astype(BF16)
        act_s[rows, :] = act
        ggp_s[rows, :] = ggp
        gup_s[rows, :] = gup
        out_ref[rows, :] += nn(act, down)
        gmid_ref[rows, :] += nt(ggp, gate) + nt(gup, up)

    ggp = ggp_s[...]
    gup = gup_s[...]

    @pl.loop(0, midt_ref.shape[0] // TILE)
    def _(t):
        rows = pl.ds(pl.multiple_of(t * TILE, TILE), TILE)
        m = midt_ref[rows, :]
        ggate_ref[rows, :] = nn(m, ggp).astype(BF16)
        gup_ref[rows, :] = nn(m, gup).astype(BF16)

    gdown_ref[...] = tn(act_s[...], cot_ref[...]).astype(BF16)


def feed(mid, midt, cot, hid, gmid, gate, up, down, steps):
    count, d = mid.shape
    args = [mid, midt, cot, hid]
    specs = [whole((count, d)), whole((d, count)), whole((count, d)), whole((count, d))]
    if gmid is None:
        body = lambda a, b, c, e, *rest: feed_kernel(a, b, c, e, None, *rest)
    else:
        body = feed_kernel
        args.append(gmid)
        specs.append(whole((count, d)))
    wide = steps * TILE
    return pl.pallas_call(
        body,
        grid=(steps,),
        in_specs=specs + [gate[1], up[1], down[1]],
        out_specs=[
            whole((count, d)),
            whole((count, d)),
            pl.BlockSpec((d, TILE), lambda i: (0, i)),
            pl.BlockSpec((d, TILE), lambda i: (0, i)),
            pl.BlockSpec((TILE, d), lambda i: (i, 0)),
        ],
        out_shape=[
            shape_of((count, d), F32),
            shape_of((count, d), F32),
            shape_of((d, wide), BF16),
            shape_of((d, wide), BF16),
            shape_of((wide, d), BF16),
        ],
        scratch_shapes=[pltpu.VMEM((count, TILE), BF16)] * 3,
        compiler_params=params(),
        name="feed",
    )(*args, gate[0], up[0], down[0])


def middle_back_kernel(
    gmid_ref, hid_ref, cot_ref, att_ref, wo_ref, gain_ref, ghid_ref, gatt_ref, go_ref, gn_ref, acc
):
    step = pl.program_id(0)

    @pl.when(step == 0)
    def _():
        acc[...] = jnp.zeros_like(acc)
        gn_ref[...] = jnp.zeros_like(gn_ref)

    hid = hid_ref[...]
    root = lax.rsqrt(jnp.mean(hid * hid, axis=-1, keepdims=True) + EPSILON)
    unit = hid * root
    gmid = gmid_ref[...]
    gn_ref[0:1, :] += jnp.sum(gmid * unit, axis=0, keepdims=True)
    t = gmid * gain_ref[1:2, :]
    inner = jnp.mean(t * unit, axis=-1, keepdims=True)
    ghid = cot_ref[...].astype(F32) + root * (t - unit * inner)
    ghid_ref[...] = ghid
    branch = ghid.astype(BF16)
    gatt_ref[...] = nt(branch, wo_ref[...]).astype(BF16)
    acc[...] += tn(att_ref[...], branch)

    @pl.when(step == pl.num_programs(0) - 1)
    def _():
        go_ref[...] = acc[...].astype(BF16)


def middle_back(gmid, hid, cot, att, wo, gains):
    count, d = hid.shape
    width = att.shape[1]
    return pl.pallas_call(
        middle_back_kernel,
        grid=(count // TILE,),
        in_specs=[
            rows_of(TILE, d),
            rows_of(TILE, d),
            rows_of(TILE, d),
            rows_of(TILE, width),
            wo[1],
            whole((8, d)),
        ],
        out_specs=[rows_of(TILE, d), rows_of(TILE, width), whole((width, d)), whole((8, d))],
        out_shape=[
            shape_of((count, d), F32),
            shape_of((count, width), BF16),
            shape_of((width, d), BF16),
            shape_of((8, d), F32),
        ],
        scratch_shapes=[pltpu.VMEM((width, d), F32)],
        compiler_params=params(),
        name="middle_back",
    )(gmid, hid, cot, att, wo[0], gains)


def project_back_kernel(
    gq_ref,
    gk_ref,
    gv_ref,
    lat_ref,
    n_ref,
    tok_ref,
    ghid_ref,
    wq_ref,
    wl_ref,
    ku_ref,
    vu_ref,
    gain_ref,
    gtok_ref,
    gwq_ref,
    gwl_ref,
    gku_ref,
    gvu_ref,
    gn_ref,
    acc_q,
    acc_l,
    acc_k,
    acc_v,
):
    step = pl.program_id(0)

    @pl.when(step == 0)
    def _():
        for ref in (acc_q, acc_l, acc_k, acc_v, gn_ref):
            ref[...] = jnp.zeros_like(ref)

    wide = ku_ref.shape[0] // G
    out = ku_ref.shape[1]
    lat = lat_ref[...]
    pieces = []
    for g in range(G):
        gk = gk_ref[:, g * out : (g + 1) * out]
        gv = gv_ref[:, g * out : (g + 1) * out]
        own = slice(g * wide, (g + 1) * wide)
        pieces.append(nt(gk, ku_ref[own, :]) + nt(gv, vu_ref[own, :]))
        acc_k[own, :] += tn(lat[:, own], gk)
        acc_v[own, :] += tn(lat[:, own], gv)
    glat = jnp.concatenate(pieces, axis=1).astype(BF16)
    gq = gq_ref[...]
    acc_q[...] += tn(n_ref[...], gq)
    acc_l[...] += tn(n_ref[...], glat)
    gin = nt(gq, wq_ref[...]) + nt(glat, wl_ref[...])
    x = tok_ref[...].astype(F32)
    root = lax.rsqrt(jnp.mean(x * x, axis=-1, keepdims=True) + EPSILON)
    unit = x * root
    gn_ref[0:1, :] += jnp.sum(gin * unit, axis=0, keepdims=True)
    t = gin * gain_ref[0:1, :]
    inner = jnp.mean(t * unit, axis=-1, keepdims=True)
    gtok_ref[...] = (ghid_ref[...] + root * (t - unit * inner)).astype(BF16)

    @pl.when(step == pl.num_programs(0) - 1)
    def _():
        gwq_ref[...] = acc_q[...].astype(BF16)
        gwl_ref[...] = acc_l[...].astype(BF16)
        gku_ref[...] = acc_k[...].astype(BF16)
        gvu_ref[...] = acc_v[...].astype(BF16)


def project_back(gq, gk, gv, lat, normed, tokens, ghid, first, ku, vu, gains):
    count, d = tokens.shape
    width = gq.shape[1]
    latw = lat.shape[1]
    return pl.pallas_call(
        project_back_kernel,
        grid=(count // TILE,),
        in_specs=[
            rows_of(TILE, width),
            rows_of(TILE, width),
            rows_of(TILE, width),
            rows_of(TILE, latw),
            rows_of(TILE, d),
            rows_of(TILE, d),
            rows_of(TILE, d),
            pl.BlockSpec((d, width), lambda i: (0, 0)),
            pl.BlockSpec((d, latw), lambda i: (0, width // latw)),
            whole(ku.shape),
            whole(vu.shape),
            whole((8, d)),
        ],
        out_specs=[
            rows_of(TILE, d),
            whole((d, width)),
            whole((d, latw)),
            whole(ku.shape),
            whole(vu.shape),
            whole((8, d)),
        ],
        out_shape=[
            shape_of((count, d), BF16),
            shape_of((d, width), BF16),
            shape_of((d, latw), BF16),
            shape_of(ku.shape, BF16),
            shape_of(vu.shape, BF16),
            shape_of((8, d), F32),
        ],
        scratch_shapes=[
            pltpu.VMEM((d, width), F32),
            pltpu.VMEM((d, latw), F32),
            pltpu.VMEM(ku.shape, F32),
            pltpu.VMEM(vu.shape, F32),
        ],
        compiler_params=params(),
        name="project_back",
    )(gq, gk, gv, lat, normed, tokens, ghid, first, first, ku, vu, gains)


def swap(values, axis_name, bit):
    size = lax.axis_size(axis_name)
    return lax.ppermute(values, axis_name, [(i, i ^ bit) for i in range(size)])


def bits_of(axis_name):
    size = lax.axis_size(axis_name)
    return [1 << i for i in range(size.bit_length() - 1)]


def owner_dims(values):
    names = [("dp", bit) for bit in reversed(bits_of("dp"))]
    names += [("fsdp", bit) for bit in reversed(bits_of("fsdp"))]
    rows = values.shape[0] >> len(names)
    return values.reshape((2,) * len(names) + (rows, values.shape[1])), names


def halve(values, names, which):
    at = names.index(which)
    axis_name, bit = which
    mine = (lax.axis_index(axis_name) // bit) % 2
    keep = lax.dynamic_index_in_dim(values, mine, at, keepdims=False)
    send = lax.dynamic_index_in_dim(values, 1 - mine, at, keepdims=False)
    came = swap(send, axis_name, bit)
    rest = names[:at] + names[at + 1 :]
    return (keep.astype(F32) + came.astype(F32)).astype(BF16), rest


def scatter_sum(values):
    split, names = owner_dims(values)
    split, names = halve(split, names, ("dp", 1))
    outer = [("dp", bit) for bit in bits_of("dp")[1:]]
    inner = [("fsdp", bit) for bit in bits_of("fsdp")]
    orders = (inner[:1] + outer + inner[1:], outer + inner)
    columns = values.shape[1]
    cut = columns // 256 * 128
    done = []
    for order, part in zip(orders, (split[..., :cut], split[..., cut:])):
        left = names
        for which in order:
            part, left = halve(part, left, which)
        done.append(part)
    return jnp.concatenate(done, axis=-1)


def shards(
    tokens,
    doc_ids,
    norm_in,
    query_weight,
    latent_weight,
    key_up_weight,
    value_up_weight,
    output_weight,
    norm_mid,
    gate_weight,
    up_weight,
    down_weight,
    cotangent,
):
    both = ("dp", "fsdp")
    devices = lax.axis_size("dp") * lax.axis_size("fsdp")
    own_rows, d = query_weight.shape
    d_all = own_rows * devices
    latw = latent_weight.shape[1]
    up_rows, up_width = key_up_weight.shape
    ff = gate_weight.shape[1]
    length = doc_ids.shape[1]

    gains = jnp.stack([norm_in, norm_mid], axis=1)
    gains = jnp.pad(gains, ((0, 0), (0, PAIR - 2)))
    packed = jnp.concatenate(
        [
            query_weight,
            latent_weight,
            jnp.concatenate([key_up_weight, value_up_weight], axis=0),
            gains,
        ],
        axis=1,
    )
    first = lax.all_gather(packed, both, axis=0, tiled=True)
    second = lax.all_gather(
        jnp.concatenate([output_weight, gate_weight, up_weight], axis=1), both, axis=0, tiled=True
    )
    down = lax.all_gather(down_weight, both, axis=0, tiled=True)

    ups = first[:, d + latw : d + latw + up_width].reshape(devices, 2, up_rows, up_width)
    ku = ups[:, 0].reshape(devices * up_rows, up_width)
    vu = ups[:, 1].reshape(devices * up_rows, up_width)

    q, lat, k, v, normed, gain_rows = project(tokens, first, ku, vu)
    att, lse = attend(doc_ids, q, k, v)
    wo = (second, pl.BlockSpec((d_all, d), lambda i: (0, 0)))
    hid, mid, midt = middle(att, wo, tokens, gain_rows)

    gate_at = d // TILE
    up_at = (d + ff) // TILE
    steps = ff // TILE
    out, gmid, ggate, gup, gdown = feed(
        mid,
        midt,
        cotangent,
        hid,
        None,
        (second, pl.BlockSpec((d_all, TILE), lambda i: (0, gate_at + i))),
        (second, pl.BlockSpec((d_all, TILE), lambda i: (0, up_at + i))),
        (down, pl.BlockSpec((TILE, d), lambda i: (i, 0))),
        steps,
    )
    layer_out = out.astype(BF16)
    ghid, gatt, go, gnorm_mid = middle_back(gmid, hid, cotangent, att, wo, gain_rows)
    gq, gk, gv = attend_back(doc_ids, q, k, v, att, gatt, lse)
    gtok, gwq, gwl, gku, gvu, gnorm_in = project_back(
        gq, gk, gv, lat, normed, tokens, ghid, first, ku, vu, gain_rows
    )
    s_gu = scatter_sum(jnp.concatenate([ggate, gup], axis=1))
    s_down = scatter_sum(gdown)
    s_o = scatter_sum(go)
    gnorms = jnp.stack([gnorm_in[0], gnorm_mid[0]], axis=1).astype(BF16)
    gups = jnp.concatenate(
        [gku.reshape(devices, up_rows, up_width), gvu.reshape(devices, up_rows, up_width)], axis=1
    ).reshape(d_all, up_width)
    s_first = scatter_sum(
        jnp.concatenate([gwq, gwl, gups, jnp.pad(gnorms, ((0, 0), (0, PAIR - 2)))], axis=1)
    )
    s_first = s_first.astype(F32)
    at = d + latw
    return (
        layer_out,
        gtok,
        s_first[:, at + up_width],
        s_first[:, :d],
        s_first[:, d:at],
        s_first[:up_rows, at : at + up_width],
        s_first[up_rows:, at : at + up_width],
        s_o.astype(F32),
        s_first[:, at + up_width + 1],
        s_gu[:, :ff].astype(F32),
        s_gu[:, ff:].astype(F32),
        s_down.astype(F32),
    )


def solution(mesh):
    split = ("dp", "fsdp")
    flat, matrix = P(split), P(split, None)
    return jax.shard_map(
        shards,
        mesh=mesh,
        in_specs=(
            matrix,
            matrix,
            flat,
            matrix,
            matrix,
            matrix,
            matrix,
            matrix,
            flat,
            matrix,
            matrix,
            matrix,
            matrix,
        ),
        out_specs=(
            matrix,
            matrix,
            flat,
            matrix,
            matrix,
            matrix,
            matrix,
            matrix,
            flat,
            matrix,
            matrix,
            matrix,
        ),
        check_vma=False,
    )
```

time: 1460 us -> 624 us (0.43)
  blocking collectives: 436 us -> 0 us
  matrix products: 395 us -> 0 us
  Pallas kernels: 0 us -> 209 us
  other arithmetic: 133 us -> 45.6 us
  local copies, waits for them, and re-layouts: 81.4 us -> 31.5 us
  starting transfers between devices: 82.6 us -> 36.8 us
  waiting for transfers between devices: 302 us -> 275 us
    dot_general x52 -> x0, matrix products: 395 us -> none  [the longest x4 49.6 us: one_block(): jnp.einsum('qhd,khd->hqk', query_heads, key_heads, preferred_element_type...]
    all_gather x4 -> x0, blocking collectives: 285 us -> none  [the longest x1 75 us: shards(): lax.all_gather(shard_key, ('dp', 'fsdp'), axis=0, tiled=True)]
    all_to_all x20 -> x0, waiting for transfers between devices: 258 us -> none  [the longest x1 60.1 us: shards(): lax.all_to_all(g7.astype(jnp.bfloat16), 'dp', split_axis=0, concat_axis=0...]
    pallas_call x0 -> x7, Pallas kernels: none -> 209 us  [the longest x1 86.8 us: feed(): pl.pallas_call(body, grid=(steps,), in_specs=specs + [gate[1], up[1], dow...]
    unnamed x2 -> x0, blocking collectives: 151 us -> none
    all_gather x12 -> x3, waiting for transfers between devices: 37.6 us -> 181 us  [the longest x1 63.1 us: shards(): first = lax.all_gather(packed, both, axis=0, tiled=True)]
    ppermute x0 -> x36, waiting for transfers between devices: none -> 93.9 us  [swap(): return lax.ppermute(values, axis_name, [(i, i ^ bit) for i in range(size)])]
    all_to_all x20 -> x0, starting transfers between devices: 82.2 us -> none  [the longest x1 5.98 us: shards(): lax.all_to_all(h6.astype(jnp.bfloat16), 'fsdp', split_axis=0, concat_axis...]
  transfers between devices with their start and end apart: 32 -> 39, of which waited for: 18 -> 26; matrix products, arithmetic and copies ran while one was open for 40% -> 10% of each run, Pallas kernels for 0% -> 8%
where the time goes in v1:
time: 624 us; the launch traced here: 613 us
  waiting for transfers between devices  275 us (44%)
  Pallas kernels  209 us (33%)
  other arithmetic  45.6 us (7%)
  starting transfers between devices  36.8 us (6%)
  local copies, waits for them, and re-layouts  31.5 us (5%)
  between operations  14.7 us (2%)
    ppermute x36, waiting for transfers between devices, swap(): return lax.ppermute(values, axis_name, [(i, i ^ bit) for i in range(size)])  93.9 us
    pallas_call x1, Pallas kernels, feed(): pl.pallas_call(body, grid=(steps,), in_specs=specs + [gate[1], up[1], dow...  86.8 us
    all_gather x1, waiting for transfers between devices, shards(): first = lax.all_gather(packed, both, axis=0, tiled=True)  63.1 us
    all_gather x1, waiting for transfers between devices, shards(): down = lax.all_gather(down_weight, both, axis=0, tiled=True)  60.2 us
    all_gather x1, waiting for transfers between devices, shards(): lax.all_gather(jnp.concatenate([output_weight, gate_weight, up_weight], a...  57.3 us
    pallas_call x1, Pallas kernels, attend_back(): pl.pallas_call(attend_back_kernel, grid_spec=pltpu.PrefetchScalarGridSpec...  40.7 us
    ppermute x36, starting transfers between devices, swap(): return lax.ppermute(values, axis_name, [(i, i ^ bit) for i in range(size)])  36.7 us
    pallas_call x1, Pallas kernels, attend(): pl.pallas_call(attend_kernel, grid_spec=pltpu.PrefetchScalarGridSpec(num_...  33.5 us
  transfers between devices with their start and end apart: 39, of which 26 were waited for; matrix products, arithmetic and copies ran while one was open for 10% of the time, Pallas kernels for 8%

profile of v1, /device:TPU:0, one launch (start us, length us, event | category | flops | bytes accessed | tf_op | source)
XLA Modules:
  0.0 613.2 jit_solution(3514176980170455101)
XLA Ops:
  14.0 63.1 %all-gather.4.cloned.1.call-done.wq_ref.wl_ref.wg_ref = bf16[1024,2176]{1,0:T(8,128)(2,1)} async-done(((bf16[32,2176]{1,0:T(8,128)(2,1)}), bf16[1024,2176]{1,0:T(8,128)(2,1)}) %all-gather.4.cloned.1.call-update) | async-done | bytes 4456464 | tf_op jit(solution)/shard_map/all_gather | solution.py:693
  79.5 9.5 %project.1 = (bf16[1024,1024]{1,0:T(8,128)(2,1)}, bf16[1024,512]{1,0:T(8,128)(2,1)}, bf16[1024,1024]{1,0:T(8,128)(2,1)}, bf16[1024,1024]{1,0:T(8,128)(2,1)}, bf1...) custom-call(bf16[1024,1024]{1,0:T(8,128)(2,1)} %tok_ref.5, ...), custom_call_target="tpu_custom_call" | custom-call | tf_op jit(solution)/shard_map/project/pallas_call | solution.py:82
  89.0 33.5 %attend.1 = (bf16[1024,1024]{1,0:T(8,128)(2,1)}, f32[8,8,1024]{2,1,0:T(8,128)}) custom-call(s32[1024]{0:T(1024)} %bitcast.237, bf16[1024,1024]{1,0:T(8,128)(2,1)} %get-tuple-element.41.q_ref, bf16[1024,1024]{1,0:T(8,128)(2,1)} %get-tuple-element.42.k_ref, bf16[1024,1024]{1,0:T(8,128)(2,1)} %get-tuple-element.43.v_ref, s32[1024,1]{1,0:T(8,128)} %copy.60.col_ref, ...), custom_call_target="tpu_custom_call" | custom-call | tf_op jit(solution)/shard_map/attend/pallas_call | solution.py:182
  122.5 57.3 %all-gather.6.cloned.1.call-done.wo_ref.rest_0_.rest_1_ = bf16[1024,6656]{1,0:T(8,128)(2,1)} async-done(((bf16[32,6656]{1,0:T(8,128)(2,1)}), bf16[1024,6656]{1,0:T(8,128)(2,1)}) %all-gather.6.cloned.1.call-update) | async-done | bytes 13631504 | tf_op jit(solution)/shard_map/all_gather | solution.py:694
  179.8 8.1 %middle.1 = (f32[1024,1024]{1,0:T(8,128)}, bf16[1024,1024]{1,0:T(8,128)(2,1)}, bf16[1024,1024]{1,0:T(8,128)(2,1)}) custom-call(bf16[1024,1024]{1,0:T(8,128)(2,1)} %get-tuple-element.44.att_ref.o_ref, bf16[1024,6656]{1,0:T(8,128)(2,1)} %all-gather.6.cloned.1.call-done.wo_ref.rest_0_.rest_1_, bf16[1024,1024]{1,0:T(8,128)(2,1)} %tok_ref.5, ...), custom_call_target="tpu_custom_call" | custom-call | tf_op jit(solution)/shard_map/middle/pallas_call | solution.py:330
  188.0 60.2 %all-gather.8.cloned.1.call-done.rest_2_ = bf16[2816,1024]{1,0:T(8,128)(2,1)} async-done(((bf16[88,1024]{1,0:T(8,128)(2,1)}), bf16[2816,1024]{1,0:T(8,128)(2,1)}) %all-gather.8.cloned.1.call-update) | async-done | bytes 5767184 | tf_op jit(solution)/shard_map/all_gather | solution.py:697
  248.2 86.8 %feed.1 = (f32[1024,1024]{1,0:T(8,128)}, f32[1024,1024]{1,0:T(8,128)}, bf16[1024,2816]{1,0:T(8,128)(2,1)}, bf16[1024,2816]{1,0:T(8,128)(2,1)}, bf16[2816,1024]{1,0:T(8,128)(2,1)}) custom-call(bf16[1024,1024]{1,0:T(8,128)(2,1)} %get-tuple-element.46.a, bf16[1024,1024]{1,0:T(8,128)(2,1)} %get-tuple-element.47.b, bf16[1024,1024]{1,0:T(8,128)(2,1)} %cot_ref.1, ...), custom_call_target="tpu_custom_call" | custom-call | tf_op jit(solution)/shard_map/feed/pallas_call | solution.py:423
  335.0 3.8 convert_element_type.455
  338.8 13.2 %middle_back.1 = (f32[1024,1024]{1,0:T(8,128)}, bf16[1024,1024]{1,0:T(8,128)(2,1)}, bf16[1024,1024]{1,0:T(8,128)(2,1)}, f32[8,1024]{1,0:T(8,128)}) custom-call(f32[1024,1024]{1,0:T(8,128)} %get-tuple-element.50.gmid_ref, f32[1024,1024]{1,0:T(8,128)} %get-tuple-element.48.e.hid_ref, bf16[1024,1024]{1,0:T(8,128)(2,1)} %cot_ref.1, ...), custom_call_target="tpu_custom_call" | custom-call | tf_op jit(solution)/shard_map/middle_back/pallas_call | solution.py:478
  352.0 40.7 %attend_back.1 = (bf16[1024,1024]{1,0:T(8,128)(2,1)}, bf16[1024,1024]{1,0:T(8,128)(2,1)}, bf16[1024,1024]{1,0:T(8,128)(2,1)}) custom-call(s32[1024]{0:T(1024)} %bitcast.238, bf16[1024,1024]{1,0:T(8,128)(2,1)} %get-tuple-element.41.q_ref, bf16[1024,1024]{1,0:T(8,128)(2,1)} %get-tuple-element.42.k_ref, bf16[1024,1024]{1,0:T(8,128)(2,1)} %get-tuple-element.43.v_ref, ...), custom_call_target="tpu_custom_call" | custom-call | tf_op jit(solution)/shard_map/attend_back/pallas_call | solution.py:294
  392.7 17.5 %project_back.1 = (bf16[1024,1024]{1,0:T(8,128)(2,1)}, bf16[1024,1024]{1,0:T(8,128)(2,1)}, bf16[1024,512]{1,0:T(8,128)(2,1)}, bf16[512,512]{1,0:T(8,128)(2,1)}, ...) custom-call(bf16[1024,1024]{1,0:T(8,128)(2,1)} %get-tuple-element.53.gq_ref, bf16[1024,1024]{1,0:T(8,128)(2,1)} %get-tuple-element.54.gk_ref, ...), custom_call_target="tpu_custom_call" | custom-call | tf_op jit(solution)/shard_map/project_back/pallas_call | solution.py:569
  419.9 16.8 %pad_maximum_fusion = bf16[1024,5632]{1,0:T(8,128)(2,1)} fusion(bf16[1024,2816]{1,0:T(8,128)(2,1)S(1)} %bitcast.223, bf16[1024,2816]{1,0:T(8,128)(2,1)S(1)} %bitcast.221), kind=kLoop, calls=%fused_computation | loop fusion | flops 23068672 | bytes 23068672 | tf_op jit(solution)/shard_map/concatenate | solution.py:728
  436.7 9.8 %constant_dynamic-slice_fusion.3 = (bf16[2,1,2,2,2,32,5632]{6,5,4,3,2,1,0:T(8,128)(2,1)}, bf16[2,1,2,2,2,32,5632]{6,5,4,3,2,1,0:T(8,128)(2,1)}) fusion(bf16[2,2,2,2,2,32,5632]{6,5,4,3,2,1,0:T(8,128)(2,1)} %bitcast.215, s32[]{:T(128)S(6)} %select_n.251, s32[]{:T(128)S(6)} %select_n.252), kind=kLoop, calls=%fused_computation.126 | loop fusion | bytes 23068680 | tf_op jit(solution)/shard_map/jit(dynamic_index_in_dim)/dynamic_slice | solution.py:634
  455.7 4.8 collective-permute-done.14
  481.6 8.6 %collective-permute-done.1 = bf16[2,2,2,32,1024]{4,3,1,2,0:T(8,128)(2,1)S(1)} collective-permute-done((bf16[2,2,2,32,1024]{4,3,1,2,0:T(8,128)(2,1)S(1)}, bf16[2,2,2,32,1024]{4,3,1,2,0:T(8,128)(2,1)S(1)}, u32[]{:S(2)}, u32[]{:S(2)}) %collective-permute-start.1) | collective-permute-done | bytes 524320 | tf_op jit(solution)/shard_map/ppermute | solution.py:615
  512.7 4.1 collective-permute-done.8
  529.5 6.0 fusion
  541.0 4.3 collective-permute-done.35
  547.1 14.7 %collective-permute-done.19 = bf16[2,2,2,32,2816]{4,3,1,2,0:T(8,128)(2,1)S(1)} collective-permute-done((bf16[2,2,2,32,2816]{4,3,1,2,0:T(8,128)(2,1)S(1)}, bf16[2,2,2,32,2816]{4,3,1,2,0:T(8,128)(2,1)S(1)}, u32[]{:S(2)}, u32[]{:S(2)}) %collective-permute-start.19) | collective-permute-done | bytes 1441824 | tf_op jit(solution)/shard_map/ppermute | solution.py:615
  563.5 13.6 %collective-permute-done.23 = bf16[2,2,2,32,2816]{4,3,0,1,2:T(8,128)(2,1)S(1)} collective-permute-done((bf16[2,2,2,32,2816]{4,3,0,1,2:T(8,128)(2,1)S(1)}, bf16[2,2,2,32,2816]{4,3,0,1,2:T(8,128)(2,1)S(1)}, u32[]{:S(2)}, u32[]{:S(2)}) %collective-permute-start.23) | collective-permute-done | bytes 1441824 | tf_op jit(solution)/shard_map/ppermute | solution.py:615
  578.3 6.4 %collective-permute-done.20 = bf16[2,2,32,2816]{3,2,0,1:T(8,128)(2,1)S(1)} collective-permute-done((bf16[2,2,32,2816]{3,2,0,1:T(8,128)(2,1)S(1)}, bf16[2,2,32,2816]{3,2,0,1:T(8,128)(2,1)S(1)}, u32[]{:S(2)}, u32[]{:S(2)}) %collective-permute-start.20) | collective-permute-done | bytes 720928 | tf_op jit(solution)/shard_map/ppermute | solution.py:615
  585.1 3.8 collective-permute-done.24
  589.1 5.3 collective-permute-done.21
  594.6 3.7 collective-permute-done.25
  (185 shorter events, 102.8 us)
Async XLA Ops:
  7.2 70.0 %all-gather.4.cloned.1.call-start = ((), (), s32[]{:S(2)}) async-start(), calls=%async_computation | async-start | bytes 4595712 | tf_op jit(solution)/shard_map/all_gather | solution.py:693
  9.6 170.2 %all-gather.6.cloned.1.call-start = ((), (), s32[]{:S(2)}) async-start(), calls=%async_computation.1 | async-start | bytes 14057472 | tf_op jit(solution)/shard_map/all_gather | solution.py:694
  11.5 236.7 %all-gather.8.cloned.1.call-start = ((), (), s32[]{:S(2)}) async-start(), calls=%async_computation.2 | async-start | bytes 5947392 | tf_op jit(solution)/shard_map/all_gather | solution.py:697
  415.9 60.6 %collective-permute-start = (bf16[2,2,2,2,32,2176]{5,4,1,2,3,0:T(8,128)(2,1)}, bf16[2,2,2,2,32,2176]{5,4,1,2,3,0:T(8,128)(2,1)}, u32[]{:S(2)}, u32[]{:S(2)}) collective-permute-start(bf16[2,2,2,2,32,2176]{5,4,1,2,3,0:T(8,128)(2,1)} %bitcast.213), channel_id=1, source_target_pairs={{0,8},{8,0},{16,24},{24,16},{1,9},{9,1},{17,25},{25,17},{2,10},{10... | collective-permute-start | bytes 6684680 | tf_op jit(solution)/shard_map/ppermute | solution.py:615
  418.1 32.0 %collective-permute-start.9 = (bf16[2,2,2,2,32,1024]{5,4,1,2,3,0:T(8,128)(2,1)}, bf16[2,2,2,2,32,1024]{5,4,1,2,3,0:T(8,128)(2,1)}, u32[]{:S(2)}, u32[]{:S(2)}) collective-permute-start(bf16[2,2,2,2,32,1024]{5,4,1,2,3,0:T(8,128)(2,1)} %bitcast.214), channel_id=1, source_target_pairs={{0,8},{8,0},{16,24},{24,16},{1,9},{9,1},{17,25},{25,17},{2,10},{10... | collective-permute-start | bytes 3145736 | tf_op jit(solution)/shard_map/ppermute | solution.py:615
  449.8 77.2 %collective-permute-start.18 = (bf16[2,2,2,2,32,5632]{5,4,1,2,3,0:T(8,128)(2,1)S(1)}, bf16[2,2,2,2,32,5632]{5,4,1,2,3,0:T(8,128)(2,1)S(1)}, u32[]{:S(2)}, u32[]{:S(2)}) collective-permute-start(bf16[2,2,2,2,32,5632]{5,4,1,2,3,0:T(8,128)(2,1)S(1)} %bitcast.216), channel_id=1, source_target_pairs={{0,8},{8,0},{16,24},{24,16},{1,9},{9,1},{17,25},{25,17},{2,10},{10... | collective-permute-start | bytes 17301512 | tf_op jit(solution)/shard_map/ppermute | solution.py:615
  452.0 8.5 %collective-permute-start.14 = (bf16[2,2,2,32,512]{4,3,0,1,2:T(8,128)(2,1)S(1)}, bf16[2,2,2,32,512]{4,3,0,1,2:T(8,128)(2,1)S(1)}, u32[]{:S(2)}, u32[]{:S(2)}) collective-permute-start(bf16[2,2,2,32,512]{4,3,0,1,2:T(8,128)(2,1)S(1)} %dynamic-slice_bitcast_fusion.13), channel_id=1, source_target_pairs={{0,16},{8,24},{16,0},{24,8},{1,17},{9,25},{17,1},{25,9},{2,18},{10... | collective-permute-start | bytes 786440 | tf_op jit(solution)/shard_map/ppermute | solution.py:615
  454.9 42.5 %collective-permute-start.27 = (bf16[2,2,2,2,88,1024]{5,4,1,2,3,0:T(8,128)(2,1)S(1)}, bf16[2,2,2,2,88,1024]{5,4,1,2,3,0:T(8,128)(2,1)S(1)}, u32[]{:S(2)}, u32[]{:S(2)}) collective-permute-start(bf16[2,2,2,2,88,1024]{5,4,1,2,3,0:T(8,128)(2,1)S(1)} %bitcast.229), channel_id=1, source_target_pairs={{0,8},{8,0},{16,24},{24,16},{1,9},{9,1},{17,25},{25,17},{2,10},{10... | collective-permute-start | bytes 8650760 | tf_op jit(solution)/shard_map/ppermute | solution.py:615
  455.1 9.2 %collective-permute-start.10 = (bf16[2,2,2,32,512]{4,3,1,2,0:T(8,128)(2,1)S(1)}, bf16[2,2,2,32,512]{4,3,1,2,0:T(8,128)(2,1)S(1)}, u32[]{:S(2)}, u32[]{:S(2)}) collective-permute-start(bf16[2,2,2,32,512]{4,3,1,2,0:T(8,128)(2,1)S(1)} %dynamic-slice_bitcast_fusion.14), channel_id=1, source_target_pairs={{0,1},{1,0},{2,3},{3,2},{4,5},{5,4},{6,7},{7,6},{8,9},{9,8},{10,11... | collective-permute-start | bytes 786440 | tf_op jit(solution)/shard_map/ppermute | solution.py:615
  478.9 11.2 %collective-permute-start.1 = (bf16[2,2,2,32,1024]{4,3,1,2,0:T(8,128)(2,1)S(1)}, bf16[2,2,2,32,1024]{4,3,1,2,0:T(8,128)(2,1)S(1)}, u32[]{:S(2)}, u32[]{:S(2)}) collective-permute-start(bf16[2,2,2,32,1024]{4,3,1,2,0:T(8,128)(2,1)S(1)} %dynamic-slice_bitcast_fusion.7), channel_id=1, source_target_pairs={{0,1},{1,0},{2,3},{3,2},{4,5},{5,4},{6,7},{7,6},{8,9},{9,8},{10,11... | collective-permute-start | bytes 1572872 | tf_op jit(solution)/shard_map/ppermute | solution.py:615
  480.0 14.4 %collective-permute-start.5 = (bf16[2,2,2,32,1152]{4,3,0,1,2:T(8,128)(2,1)S(1)}, bf16[2,2,2,32,1152]{4,3,0,1,2:T(8,128)(2,1)S(1)}, u32[]{:S(2)}, u32[]{:S(2)}) collective-permute-start(bf16[2,2,2,32,1152]{4,3,0,1,2:T(8,128)(2,1)S(1)} %dynamic-slice_bitcast_fusion.6), channel_id=1, source_target_pairs={{0,16},{8,24},{16,0},{24,8},{1,17},{9,25},{17,1},{25,9},{2,18},{10... | collective-permute-start | bytes 1769480 | tf_op jit(solution)/shard_map/ppermute | solution.py:615
  490.4 10.3 %collective-permute-start.2 = (bf16[2,2,32,1024]{3,2,0,1:T(8,128)(2,1)S(1)}, bf16[2,2,32,1024]{3,2,0,1:T(8,128)(2,1)S(1)}, u32[]{:S(2)}, u32[]{:S(2)}) collective-permute-start(bf16[2,2,32,1024]{3,2,0,1:T(8,128)(2,1)S(1)} %dynamic-slice_bitcast_fusion.15), channel_id=1, source_target_pairs={{0,16},{8,24},{16,0},{24,8},{1,17},{9,25},{17,1},{25,9},{2,18},{10... | collective-permute-start | bytes 786440 | tf_op jit(solution)/shard_map/ppermute | solution.py:615
  494.5 10.8 %collective-permute-start.6 = (bf16[2,2,32,1152]{3,2,0,1:T(8,128)(2,1)S(1)}, bf16[2,2,32,1152]{3,2,0,1:T(8,128)(2,1)S(1)}, u32[]{:S(2)}, u32[]{:S(2)}) collective-permute-start(bf16[2,2,32,1152]{3,2,0,1:T(8,128)(2,1)S(1)} %dynamic-slice_bitcast_fusion.12), channel_id=1, source_target_pairs={{0,1},{1,0},{2,3},{3,2},{4,5},{5,4},{6,7},{7,6},{8,9},{9,8},{10,11... | collective-permute-start | bytes 884744 | tf_op jit(solution)/shard_map/ppermute | solution.py:615
  499.2 17.6 %collective-permute-start.32 = (bf16[2,2,2,88,512]{4,3,0,1,2:T(8,128)(2,1)S(1)}, bf16[2,2,2,88,512]{4,3,0,1,2:T(8,128)(2,1)S(1)}, u32[]{:S(2)}, u32[]{:S(2)}) collective-permute-start(bf16[2,2,2,88,512]{4,3,0,1,2:T(8,128)(2,1)S(1)} %dynamic-slice_bitcast_fusion.2), channel_id=1, source_target_pairs={{0,16},{8,24},{16,0},{24,8},{1,17},{9,25},{17,1},{25,9},{2,18},{10... | collective-permute-start | bytes 2162696 | tf_op jit(solution)/shard_map/ppermute | solution.py:615
  499.4 19.1 %collective-permute-start.28 = (bf16[2,2,2,88,512]{4,3,1,2,0:T(8,128)(2,1)S(1)}, bf16[2,2,2,88,512]{4,3,1,2,0:T(8,128)(2,1)S(1)}, u32[]{:S(2)}, u32[]{:S(2)}) collective-permute-start(bf16[2,2,2,88,512]{4,3,1,2,0:T(8,128)(2,1)S(1)} %dynamic-slice_bitcast_fusion.3), channel_id=1, source_target_pairs={{0,1},{1,0},{2,3},{3,2},{4,5},{5,4},{6,7},{7,6},{8,9},{9,8},{10,11... | collective-permute-start | bytes 2162696 | tf_op jit(solution)/shard_map/ppermute | solution.py:615
  517.1 7.5 %collective-permute-start.33 = (bf16[2,2,88,512]{3,2,0,1:T(8,128)(2,1)S(1)}, bf16[2,2,88,512]{3,2,0,1:T(8,128)(2,1)S(1)}, u32[]{:S(2)}, u32[]{:S(2)}) collective-permute-start(bf16[2,2,88,512]{3,2,0,1:T(8,128)(2,1)S(1)} %dynamic-slice_bitcast_fusion.8), channel_id=1, source_target_pairs={{0,1},{1,0},{2,3},{3,2},{4,5},{5,4},{6,7},{7,6},{8,9},{9,8},{10,11... | collective-permute-start | bytes 1081352 | tf_op jit(solution)/shard_map/ppermute | solution.py:615
  524.8 13.1 %collective-permute-start.34 = (bf16[2,88,512]{2,1,0:T(8,128)(2,1)S(1)}, bf16[2,88,512]{2,1,0:T(8,128)(2,1)S(1)}, u32[]{:S(2)}, u32[]{:S(2)}) collective-permute-start(bf16[2,88,512]{2,1,0:T(8,128)(2,1)S(1)} %dynamic-slice_bitcast_fusion.16), channel_id=1, source_target_pairs={{0,2},{1,3},{2,0},{3,1},{4,6},{5,7},{6,4},{7,5},{8,10},{9,11},{10,... | collective-permute-start | bytes 540680 | tf_op jit(solution)/shard_map/ppermute | solution.py:615
  526.4 12.6 %collective-permute-start.30 = (bf16[2,88,512]{2,1,0:T(8,128)(2,1)S(1)}, bf16[2,88,512]{2,1,0:T(8,128)(2,1)S(1)}, u32[]{:S(2)}, u32[]{:S(2)}) collective-permute-start(bf16[2,88,512]{2,1,0:T(8,128)(2,1)S(1)} %dynamic-slice_bitcast_fusion.17), channel_id=1, source_target_pairs={{0,2},{1,3},{2,0},{3,1},{4,6},{5,7},{6,4},{7,5},{8,10},{9,11},{10,... | collective-permute-start | bytes 540680 | tf_op jit(solution)/shard_map/ppermute | solution.py:615
  536.4 25.4 %collective-permute-start.19 = (bf16[2,2,2,32,2816]{4,3,1,2,0:T(8,128)(2,1)S(1)}, bf16[2,2,2,32,2816]{4,3,1,2,0:T(8,128)(2,1)S(1)}, u32[]{:S(2)}, u32[]{:S(2)}) collective-permute-start(bf16[2,2,2,32,2816]{4,3,1,2,0:T(8,128)(2,1)S(1)} %dynamic-slice_bitcast_fusion.1), channel_id=1, source_target_pairs={{0,1},{1,0},{2,3},{3,2},{4,5},{5,4},{6,7},{7,6},{8,9},{9,8},{10,11... | collective-permute-start | bytes 4325384 | tf_op jit(solution)/shard_map/ppermute | solution.py:615
  545.5 31.6 %collective-permute-start.23 = (bf16[2,2,2,32,2816]{4,3,0,1,2:T(8,128)(2,1)S(1)}, bf16[2,2,2,32,2816]{4,3,0,1,2:T(8,128)(2,1)S(1)}, u32[]{:S(2)}, u32[]{:S(2)}) collective-permute-start(bf16[2,2,2,32,2816]{4,3,0,1,2:T(8,128)(2,1)S(1)} %dynamic-slice_bitcast_fusion), channel_id=1, source_target_pairs={{0,16},{8,24},{16,0},{24,8},{1,17},{9,25},{17,1},{25,9},{2,18},{10... | collective-permute-start | bytes 4325384 | tf_op jit(solution)/shard_map/ppermute | solution.py:615
  562.2 22.5 %collective-permute-start.20 = (bf16[2,2,32,2816]{3,2,0,1:T(8,128)(2,1)S(1)}, bf16[2,2,32,2816]{3,2,0,1:T(8,128)(2,1)S(1)}, u32[]{:S(2)}, u32[]{:S(2)}) collective-permute-start(bf16[2,2,32,2816]{3,2,0,1:T(8,128)(2,1)S(1)} %dynamic-slice_bitcast_fusion.5), channel_id=1, source_target_pairs={{0,16},{8,24},{16,0},{24,8},{1,17},{9,25},{17,1},{25,9},{2,18},{10... | collective-permute-start | bytes 2162696 | tf_op jit(solution)/shard_map/ppermute | solution.py:615
  577.5 11.4 %collective-permute-start.24 = (bf16[2,2,32,2816]{3,2,0,1:T(8,128)(2,1)S(1)}, bf16[2,2,32,2816]{3,2,0,1:T(8,128)(2,1)S(1)}, u32[]{:S(2)}, u32[]{:S(2)}) collective-permute-start(bf16[2,2,32,2816]{3,2,0,1:T(8,128)(2,1)S(1)} %dynamic-slice_bitcast_fusion.4), channel_id=1, source_target_pairs={{0,1},{1,0},{2,3},{3,2},{4,5},{5,4},{6,7},{7,6},{8,9},{9,8},{10,11... | collective-permute-start | bytes 2162696 | tf_op jit(solution)/shard_map/ppermute | solution.py:615
  585.0 9.4 %collective-permute-start.21 = (bf16[2,32,2816]{2,1,0:T(8,128)(2,1)S(1)}, bf16[2,32,2816]{2,1,0:T(8,128)(2,1)S(1)}, u32[]{:S(2)}, u32[]{:S(2)}) collective-permute-start(bf16[2,32,2816]{2,1,0:T(8,128)(2,1)S(1)} %dynamic-slice_bitcast_fusion.11), channel_id=1, source_target_pairs={{0,2},{1,3},{2,0},{3,1},{4,6},{5,7},{6,4},{7,5},{8,10},{9,11},{10,... | collective-permute-start | bytes 1081352 | tf_op jit(solution)/shard_map/ppermute | solution.py:615
  589.0 9.2 %collective-permute-start.25 = (bf16[2,32,2816]{2,1,0:T(8,128)(2,1)S(1)}, bf16[2,32,2816]{2,1,0:T(8,128)(2,1)S(1)}, u32[]{:S(2)}, u32[]{:S(2)}) collective-permute-start(bf16[2,32,2816]{2,1,0:T(8,128)(2,1)S(1)} %dynamic-slice_bitcast_fusion.10), channel_id=1, source_target_pairs={{0,2},{1,3},{2,0},{3,1},{4,6},{5,7},{6,4},{7,5},{8,10},{9,11},{10,... | collective-permute-start | bytes 1081352 | tf_op jit(solution)/shard_map/ppermute | solution.py:615
  (23 other events, 132.0 us)
Sparse Core Ops, SparseCore 0:
  11.4 65.7 all-gather.3
  80.7 99.1 all-gather.5
  182.8 65.3 all-gather.7

commit v2 on v1

v2 whole, which is shorter than its diff:
```python
import functools

import jax
import jax.numpy as jnp
from jax import lax
from jax.experimental import pallas as pl
from jax.experimental.pallas import tpu as pltpu
from jax.sharding import PartitionSpec as P

HD = 64
G = 2
HG = 8
PAIR = 128
EPSILON = 1e-05
SCORE_SCALE = 0.125
NEGATIVE = -1e30
LOG2E = 1.4426950408889634
F32 = jnp.float32
BF16 = jnp.bfloat16
TILE = 256
QT = 128
SPAN = 4
PP = 2
PPB = 2
VMEM_LIMIT = 60 * 1024 * 1024


def nn(a, b):
    return lax.dot_general(a, b, (((1,), (0,)), ((), ())), preferred_element_type=F32)


def nt(a, b):
    return lax.dot_general(a, b, (((1,), (1,)), ((), ())), preferred_element_type=F32)


def tn(a, b):
    return lax.dot_general(a, b, (((0,), (0,)), ((), ())), preferred_element_type=F32)


def params(**extra):
    return pltpu.CompilerParams(vmem_limit_bytes=VMEM_LIMIT, **extra)


def whole(shape):
    return pl.BlockSpec(shape, lambda *_: (0,) * len(shape))


def rows_of(tile, width):
    return pl.BlockSpec((tile, width), lambda i: (i, 0))


def cost(micros):
    return pl.CostEstimate(flops=int(micros * 1.1e9), bytes_accessed=0, transcendentals=0)


def shape_of(shape, dtype):
    return jax.ShapeDtypeStruct(shape, dtype)


def project_kernel(
    tok_ref,
    wq_ref,
    wl_ref,
    wg_ref,
    ku_ref,
    vu_ref,
    q_ref,
    lat_ref,
    latt_ref,
    k_ref,
    v_ref,
    nt_ref,
    gain_ref,
):
    @pl.when(pl.program_id(0) == 0)
    def _():
        gain_ref[...] = wg_ref[...].astype(F32).T[0:8, :]

    x = tok_ref[...].astype(F32)
    root = lax.rsqrt(jnp.mean(x * x, axis=-1, keepdims=True) + EPSILON)
    normed = (x * root * gain_ref[0:1, :]).astype(BF16)
    nt_ref[...] = normed.T
    lat = nn(normed, wl_ref[...]).astype(BF16)
    lat_ref[...] = lat
    latt_ref[...] = lat.T
    q_ref[...] = (nn(normed, wq_ref[...]).astype(BF16).astype(F32) * SCORE_SCALE).astype(BF16)
    wide = lat.shape[1] // G
    out = k_ref.shape[1] // G
    for g in range(G):
        piece = lat[:, g * wide : (g + 1) * wide]
        k_ref[:, g * out : (g + 1) * out] = nn(
            piece, ku_ref[g * wide : (g + 1) * wide, :]
        ).astype(BF16)
        v_ref[:, g * out : (g + 1) * out] = nn(
            piece, vu_ref[g * wide : (g + 1) * wide, :]
        ).astype(BF16)


def columns_of(height, tile):
    return pl.BlockSpec((height, tile), lambda i: (0, i))


def project(tokens, first, ku, vu):
    count, d = tokens.shape
    latw = ku.shape[0]
    width = G * ku.shape[1]
    return pl.pallas_call(
        project_kernel,
        grid=(count // TILE,),
        in_specs=[
            rows_of(TILE, d),
            pl.BlockSpec((d, width), lambda i: (0, 0)),
            pl.BlockSpec((d, latw), lambda i: (0, (width + d) // latw)),
            pl.BlockSpec((d, PAIR), lambda i: (0, (width + d + 2 * latw) // PAIR)),
            whole(ku.shape),
            whole(vu.shape),
        ],
        out_specs=[
            rows_of(TILE, width),
            rows_of(TILE, latw),
            columns_of(latw, TILE),
            rows_of(TILE, width),
            rows_of(TILE, width),
            columns_of(d, TILE),
            whole((8, d)),
        ],
        out_shape=[
            shape_of((count, width), BF16),
            shape_of((count, latw), BF16),
            shape_of((latw, count), BF16),
            shape_of((count, width), BF16),
            shape_of((count, width), BF16),
            shape_of((d, count), BF16),
            shape_of((8, d), F32),
        ],
        cost_estimate=cost(10),
        compiler_params=params(),
        name="project",
    )(tokens, first, first, first, ku, vu)


def visible(doc):
    length = doc.shape[1]
    ids = doc.reshape(length)
    blocks = []
    padded = jnp.concatenate([jnp.full((SPAN * QT,), -1, ids.dtype), ids])
    for b in range(length // QT):
        keys = jnp.arange((b - SPAN) * QT, (b + 1) * QT)
        own = ids[b * QT : (b + 1) * QT]
        theirs = padded[b * QT : (b + SPAN + 1) * QT]
        queries = jnp.arange(b * QT, (b + 1) * QT)
        seen = (theirs[:, None] == own[None, :]) & (keys[:, None] <= queries[None, :])
        blocks.append(jnp.where(seen, 0.0, NEGATIVE))
    return jnp.stack(blocks).astype(BF16)


def split_heads(values):
    low = lax.broadcasted_iota(jnp.int32, values.shape, 1) < HD
    zero = jnp.zeros_like(values)
    return jnp.concatenate([jnp.where(low, values, zero), jnp.where(low, zero, values)], axis=0)


def attend_kernel(q_ref, k_ref, v_ref, mask_ref, o_ref, ot_ref, lse_ref):
    length = q_ref.shape[0]
    low = lax.broadcasted_iota(jnp.int32, (QT, PAIR), 1) < HD
    for b in range(length // QT):
        rows = slice(b * QT, (b + 1) * QT)
        extra = min(b, SPAN)
        keys = slice((b - extra) * QT, (b + 1) * QT)
        bias = mask_ref[b, (SPAN - extra) * QT :, :].astype(F32)
        bias = jnp.concatenate([bias, bias], axis=1)
        for pair in range(PP):
            cols = slice(pair * PAIR, (pair + 1) * PAIR)
            s = nt(k_ref[keys, cols], split_heads(q_ref[rows, cols])) * LOG2E + bias
            top = jnp.max(s, axis=0, keepdims=True)
            p = jnp.exp2(s - top).astype(BF16)
            v = v_ref[keys, cols]
            r = tn(p, jnp.concatenate([v, jnp.ones_like(v)], axis=1))
            r = jnp.where(
                jnp.concatenate([low, low], axis=1), r[:QT], r[QT:]
            )
            o = r[:, :PAIR] / r[:, PAIR:]
            o_ref[rows, cols] = o.astype(BF16)
            ot_ref[cols, rows] = o.T.astype(BF16)
            total = jnp.log2(r[:, PAIR:].T)
            lse_ref[pair, 0:1, rows] = top[:, :QT] + total[0:1]
            lse_ref[pair, 1:2, rows] = top[:, QT:] + total[HD : HD + 1]


def attend(mask, q, k, v, start, pairs):
    length = q.shape[0]
    width = pairs * PAIR
    wide = PP * PAIR
    strip = pl.BlockSpec((length, wide), lambda i: (0, start // PP + i))
    return pl.pallas_call(
        attend_kernel,
        grid_spec=pltpu.PrefetchScalarGridSpec(
            num_scalar_prefetch=0,
            grid=(pairs // PP,),
            in_specs=[strip, strip, strip, whole(mask.shape)],
            out_specs=[
                pl.BlockSpec((length, wide), lambda i: (0, i)),
                pl.BlockSpec((wide, length), lambda i: (i, 0)),
                pl.BlockSpec((PP, 8, length), lambda i: (i, 0, 0)),
            ],
        ),
        out_shape=[
            shape_of((length, width), BF16),
            shape_of((width, length), BF16),
            shape_of((pairs, 8, length), F32),
        ],
        cost_estimate=cost(2.5 * pairs),
        compiler_params=params(),
        name="attend",
    )(q, k, v, mask)


def attend_back_kernel(
    q_ref,
    k_ref,
    v_ref,
    o_ref,
    do_ref,
    lse_ref,
    mask_ref,
    dq_ref,
    dk_ref,
    dv_ref,
    dk_acc,
    dv_acc,
):
    length = q_ref.shape[0]
    low = lax.broadcasted_iota(jnp.int32, (QT, PAIR), 1) < HD
    dk_acc[...] = jnp.zeros_like(dk_acc)
    dv_acc[...] = jnp.zeros_like(dv_acc)
    kts = [k_ref[:, pair * PAIR : (pair + 1) * PAIR].T for pair in range(PPB)]
    for b in range(length // QT):
        rows = slice(b * QT, (b + 1) * QT)
        extra = min(b, SPAN)
        keys = slice((b - extra) * QT, (b + 1) * QT)
        bias = mask_ref[b, (SPAN - extra) * QT :, :].astype(F32)
        bias = jnp.concatenate([bias, bias], axis=1)
        for pair in range(PPB):
            cols = slice(pair * PAIR, (pair + 1) * PAIR)
            do = do_ref[rows, cols]
            prod = (do.astype(F32) * o_ref[rows, cols].astype(F32)).T
            inner = jnp.concatenate(
                [
                    jnp.sum(prod[:HD], axis=0, keepdims=True),
                    jnp.sum(prod[HD:], axis=0, keepdims=True),
                ],
                axis=1,
            )
            lse = jnp.concatenate(
                [lse_ref[pair, 0:1, rows], lse_ref[pair, 1:2, rows]], axis=1
            )
            qs = split_heads(q_ref[rows, cols])
            dos = split_heads(do)
            k = k_ref[keys, cols]
            p = jnp.exp2(nt(k, qs) * LOG2E + bias - lse)
            ds = (p * (nt(v_ref[keys, cols], dos) - inner)).astype(BF16)
            dv_acc[keys, cols] += nn(p.astype(BF16), dos)
            dk_acc[keys, cols] += nn(ds, qs)
            dq = nn(kts[pair][:, keys], ds) * SCORE_SCALE
            dq = jnp.concatenate([dq[:HD, :QT], dq[HD:, QT:]], axis=0)
            dq_ref[rows, cols] = dq.T.astype(BF16)
    dk_ref[...] = dk_acc[...].astype(BF16)
    dv_ref[...] = dv_acc[...].astype(BF16)


def attend_back(mask, q, k, v, o, do, lse, start, at, pairs):
    length = q.shape[0]
    width = pairs * PAIR
    wide = PPB * PAIR
    strip = pl.BlockSpec((length, wide), lambda i: (0, start // PPB + i))
    own = pl.BlockSpec((length, wide), lambda i: (0, i))
    return pl.pallas_call(
        attend_back_kernel,
        grid_spec=pltpu.PrefetchScalarGridSpec(
            num_scalar_prefetch=0,
            grid=(pairs // PPB,),
            in_specs=[
                strip,
                strip,
                strip,
                pl.BlockSpec((length, wide), lambda i: (0, at // PPB + i)),
                strip,
                pl.BlockSpec((PPB, 8, length), lambda i: (at // PPB + i, 0, 0)),
                whole(mask.shape),
            ],
            out_specs=[own] * 3,
            scratch_shapes=[
                pltpu.VMEM((length, wide), F32),
                pltpu.VMEM((length, wide), F32),
            ],
        ),
        out_shape=[shape_of((length, width), BF16)] * 3,
        cost_estimate=cost(3.5 * pairs),
        compiler_params=params(),
        name="attend_back",
    )(q, k, v, o, do, lse, mask)


def middle_kernel(*refs):
    att_refs = refs[:-6]
    wo_ref, tok_ref, gain_ref, hid_ref, mid_ref, midt_ref = refs[-6:]
    att = jnp.concatenate([ref[...] for ref in att_refs], axis=1)
    hid = tok_ref[...].astype(F32) + nn(att, wo_ref[...])
    hid_ref[...] = hid
    root = lax.rsqrt(jnp.mean(hid * hid, axis=-1, keepdims=True) + EPSILON)
    mid = (hid * root * gain_ref[1:2, :]).astype(BF16)
    mid_ref[...] = mid
    midt_ref[...] = mid.T


def middle(att, wo, tokens, gains):
    count, d = tokens.shape
    return pl.pallas_call(
        middle_kernel,
        grid=(count // TILE,),
        in_specs=[rows_of(TILE, x.shape[1]) for x in att]
        + [wo[1], rows_of(TILE, d), whole((8, d))],
        out_specs=[rows_of(TILE, d), rows_of(TILE, d), columns_of(d, TILE)],
        out_shape=[
            shape_of((count, d), F32),
            shape_of((count, d), BF16),
            shape_of((d, count), BF16),
        ],
        cost_estimate=cost(8),
        compiler_params=params(),
        name="middle",
    )(*att, wo[0], tokens, gains)


def unfold_kernel(own_rows, down_rows, in_ref, out_ref):
    d = out_ref.shape[1]
    for device in range(in_ref.shape[0] // own_rows):
        for fold in range(in_ref.shape[1] // d):
            count = min(own_rows, down_rows - fold * own_rows)
            at = device * down_rows + fold * own_rows
            out_ref[at : at + count, :] = in_ref[
                device * own_rows : device * own_rows + count, fold * d : (fold + 1) * d
            ]


def unfold(wide, own_rows, down_rows, d):
    folds = -(-down_rows // own_rows)
    devices = wide.shape[0] // own_rows
    if own_rows % 16 or devices % 8:
        down = wide[:, : folds * d].reshape(devices, own_rows, folds, d).transpose(0, 2, 1, 3)
        down = down.reshape(devices, folds * own_rows, d)[:, :down_rows]
        return down.reshape(devices * down_rows, d)
    return pl.pallas_call(
        functools.partial(unfold_kernel, own_rows, down_rows),
        grid=(devices // 8,),
        in_specs=[pl.BlockSpec((8 * own_rows, folds * d), lambda i: (i, 0))],
        out_specs=pl.BlockSpec((8 * down_rows, d), lambda i: (i, 0)),
        out_shape=shape_of((devices * down_rows, d), BF16),
        cost_estimate=cost(5),
        compiler_params=params(),
        name="unfold",
    )(wide)


def owner_rows(core_ref, pair, height, mine, span=None):
    core = core_ref[0]
    first = 2 * pair if span is None else 2 * pair % span
    which = first + (core if mine else 1 - core)
    return pl.ds(pl.multiple_of(which * height, height), height)


def feed_kernel(first, last, core_ref, *refs):
    refs = list(refs)
    mid_ref, midt_ref, cot_ref, from_ref = refs[:4]
    del refs[:4]
    gfrom_ref = None
    if not first:
        gfrom_ref = refs[0]
        del refs[:2]
    gate_ref, up_ref, down_ref, out_ref, gmid_ref, keep_ref, send_ref, gdown_ref = refs[:8]
    out_acc, gmid_acc, act_s, ggp_s, gup_s = refs[8:]
    count = mid_ref.shape[0]

    @pl.when(pl.program_id(0) == 0)
    def _():
        out_acc[...] = from_ref[...]
        if first:
            gmid_acc[...] = jnp.zeros_like(gmid_acc)
        else:
            gmid_acc[...] = gfrom_ref[...]

    gate = gate_ref[...]
    up = up_ref[...]
    down = down_ref[...]
    step = 1024

    @pl.loop(0, count // step)
    def _(t):
        rows = pl.ds(pl.multiple_of(t * step, step), step)
        m = mid_ref[rows, :]
        gate_pre = nn(m, gate)
        up_pre = nn(m, up)
        grad_act = nt(cot_ref[rows, :], down)
        sig = 0.5 * jnp.tanh(0.5 * gate_pre) + 0.5
        silu = gate_pre * sig
        act = (silu * up_pre).astype(BF16)
        ggp = (grad_act * up_pre * (sig + silu * (1.0 - sig))).astype(BF16)
        gup = (grad_act * silu).astype(BF16)
        act_s[rows, :] = act
        ggp_s[rows, :] = ggp
        gup_s[rows, :] = gup
        out_acc[rows, :] += nn(act, down)
        gmid_acc[rows, :] += nt(ggp, gate) + nt(gup, up)

    ggp = ggp_s[...]
    gup = gup_s[...]
    _, pairs, height, _ = keep_ref.shape

    for mine, ref in ((False, send_ref), (True, keep_ref)):
        m = jnp.concatenate([midt_ref[owner_rows(core_ref, p, height, mine), :] for p in range(pairs)], axis=0)
        ref[0] = nn(m, ggp).astype(BF16).reshape(ref.shape[1:])
        ref[1] = nn(m, gup).astype(BF16).reshape(ref.shape[1:])

    gdown = tn(act_s[...], cot_ref[...]).astype(BF16)
    half = gdown.shape[1] // 2
    gdown_ref[0] = gdown[:, :half]
    gdown_ref[1] = gdown[:, half:]

    @pl.when(pl.program_id(0) == pl.num_programs(0) - 1)
    def _():
        out_ref[...] = out_acc[...].astype(out_ref.dtype)
        gmid_ref[...] = gmid_acc[...]


def feed(core, mid, midt, cot, start, before, gate, up, down, span, lead, n_dp, ff):
    count, d = mid.shape
    first, last = before is None, span[1] * TILE == ff
    at, steps = span[0], span[1] - span[0]
    args = [mid, midt, cot, start]
    specs = [whole((count, d)), whole((d, count)), whole((count, d)), whole((count, d))]
    alias = {}
    if not first:
        args += list(before)
        specs += [whole((count, d)), pl.BlockSpec(memory_space=pl.ANY)]
        alias = {6: 4}
    height = d // n_dp
    strip = pl.BlockSpec((2, n_dp // 2, height, TILE), lambda i, *_: (0, 0, 0, i + lead // TILE))
    grads = shape_of((2, n_dp // 2, height, lead + steps * TILE), BF16)
    return pl.pallas_call(
        functools.partial(feed_kernel, first, last),
        grid_spec=pltpu.PrefetchScalarGridSpec(
            num_scalar_prefetch=1,
            grid=(steps,),
            in_specs=specs
            + [
                pl.BlockSpec((d, TILE), lambda i, *_: (0, gate[1] + at + i)),
                pl.BlockSpec((d, TILE), lambda i, *_: (0, up[1] + at + i)),
                pl.BlockSpec((TILE, d), lambda i, *_: (at + i, 0)),
            ],
            out_specs=[
                whole((count, d)),
                whole((count, d)),
                strip,
                strip,
                pl.BlockSpec((2, TILE, d // 2), lambda i, *_: (0, at + i, 0)),
            ],
            scratch_shapes=[pltpu.VMEM((count, d), F32)] * 2
            + [pltpu.VMEM((count, TILE), BF16)] * 3,
        ),
        out_shape=[
            shape_of((count, d), BF16 if last else F32),
            shape_of((count, d), F32),
            grads,
            grads,
            shape_of((2, ff, d // 2), BF16),
        ],
        input_output_aliases=alias,
        cost_estimate=cost(7.5 * steps),
        compiler_params=params(),
        name="feed",
    )(core, *args, gate[0], up[0], down)


def middle_back_kernel(
    core_ref,
    gmid_ref,
    hid_ref,
    cot_ref,
    *refs,
):
    attt_refs = refs[:-10]
    (
        wo_ref,
        gain_ref,
        keep_in,
        send_in,
        ghid_ref,
        gatt_ref,
        keep_ref,
        send_ref,
        gn_ref,
        branch_s,
    ) = refs[-10:]
    step = pl.program_id(0)
    tile = hid_ref.shape[0]

    @pl.when(step == 0)
    def _():
        gn_ref[...] = jnp.zeros_like(gn_ref)

    hid = hid_ref[...]
    root = lax.rsqrt(jnp.mean(hid * hid, axis=-1, keepdims=True) + EPSILON)
    unit = hid * root
    gmid = gmid_ref[...]
    gn_ref[0:1, :] += jnp.sum(gmid * unit, axis=0, keepdims=True)
    t = gmid * gain_ref[1:2, :]
    inner = jnp.mean(t * unit, axis=-1, keepdims=True)
    ghid = cot_ref[...].astype(F32) + root * (t - unit * inner)
    ghid_ref[...] = ghid
    branch = ghid.astype(BF16)
    gatt_ref[...] = nt(branch, wo_ref[...]).astype(BF16)
    branch_s[pl.ds(pl.multiple_of(step * tile, tile), tile), :] = branch

    @pl.when(step == pl.num_programs(0) - 1)
    def _():
        half = branch_s.shape[1] // 2
        _, pairs, height, _ = keep_ref.shape
        tall = attt_refs[0].shape[0]
        for p in range(pairs):
            for mine, ref in ((False, send_ref), (True, keep_ref)):
                attt_ref = attt_refs[2 * p * height // tall]
                rows = attt_ref[owner_rows(core_ref, p, height, mine, tall // height), :]
                grad = nn(rows, branch_s[...]).astype(BF16)
                ref[0, p] = grad[:, :half]
                ref[1, p] = grad[:, half:]


def middle_back(core, gmid, hid, cot, attt, wo, gains, keep, send):
    count, d = hid.shape
    width = sum(x.shape[0] for x in attt)
    pairs, height = keep.shape[1:3]
    anywhere = pl.BlockSpec(memory_space=pl.ANY)
    strip = pl.BlockSpec((2, pairs, height, d // 2), lambda i, *_: (0, 0, 0, 0))
    tile = lambda wide: pl.BlockSpec((TILE, wide), lambda i, *_: (i, 0))
    return pl.pallas_call(
        middle_back_kernel,
        grid_spec=pltpu.PrefetchScalarGridSpec(
            num_scalar_prefetch=1,
            grid=(count // TILE,),
            in_specs=[
                tile(d),
                tile(d),
                tile(d),
            ]
            + [whole(x.shape) for x in attt]
            + [
                wo[1],
                whole((8, d)),
                anywhere,
                anywhere,
            ],
            out_specs=[tile(d), tile(width), strip, strip, whole((8, d))],
            scratch_shapes=[pltpu.VMEM((count, d), BF16)],
        ),
        out_shape=[
            shape_of((count, d), F32),
            shape_of((count, width), BF16),
            shape_of(keep.shape, BF16),
            shape_of(send.shape, BF16),
            shape_of((8, d), F32),
        ],
        input_output_aliases={6 + len(attt): 2, 7 + len(attt): 3},
        cost_estimate=cost(12),
        compiler_params=params(),
        name="middle_back",
    )(core, gmid, hid, cot, *attt, wo[0], gains, keep, send)


def interleave(up_rows, height):
    to = lax.broadcasted_iota(jnp.int32, (height, height), 0)
    start = lax.broadcasted_iota(jnp.int32, (height, height), 1)
    turn, row = to // (2 * up_rows), to % (2 * up_rows)
    late = (row >= up_rows).astype(jnp.int32)
    want = turn * up_rows + row - late * up_rows + late * (height // 2)
    return (start == want).astype(F32).astype(BF16)


def project_back_kernel(
    up_rows,
    core_ref,
    *refs,
):
    parts = (len(refs) - 17) // 3
    gq_refs, gk_refs, gv_refs = refs[:parts], refs[parts : 2 * parts], refs[2 * parts : 3 * parts]
    (
        latt_ref,
        nt_ref,
        tok_ref,
        ghid_ref,
        wq_ref,
        wl_ref,
        ku_ref,
        vu_ref,
        gain_ref,
        gn_mid_ref,
        gtok_ref,
        keep_ref,
        send_ref,
        glat_s,
        gn_s,
        gku_s,
        gvu_s,
    ) = refs[3 * parts :]
    step = pl.program_id(0)
    tile = tok_ref.shape[0]
    rows = pl.ds(pl.multiple_of(step * tile, tile), tile)

    @pl.when(step == 0)
    def _():
        gn_s[...] = jnp.zeros_like(gn_s)

    wide = ku_ref.shape[0] // G
    out = ku_ref.shape[1]
    each = parts // G
    strip = out // each
    pieces = []
    gin = jnp.zeros(tok_ref.shape, F32)
    for g in range(G):
        own = slice(g * wide, (g + 1) * wide)
        glat = jnp.zeros((tile, wide), F32)
        for j in range(each):
            part = g * each + j
            cols = slice(j * strip, (j + 1) * strip)
            glat += nt(gk_refs[part][rows, :], ku_ref[own, cols])
            glat += nt(gv_refs[part][rows, :], vu_ref[own, cols])
            gin += nt(gq_refs[part][rows, :], wq_ref[:, part * strip : (part + 1) * strip])
        pieces.append(glat)
    glat = jnp.concatenate(pieces, axis=1).astype(BF16)
    glat_s[rows, :] = glat
    gin += nt(glat, wl_ref[...])
    x = tok_ref[...].astype(F32)
    root = lax.rsqrt(jnp.mean(x * x, axis=-1, keepdims=True) + EPSILON)
    unit = x * root
    gn_s[0:1, :] += jnp.sum(gin * unit, axis=0, keepdims=True)
    t = gin * gain_ref[0:1, :]
    inner = jnp.mean(t * unit, axis=-1, keepdims=True)
    gtok_ref[...] = (ghid_ref[...] + root * (t - unit * inner)).astype(BF16)

    @pl.when(step == pl.num_programs(0) - 1)
    def _():
        _, pairs, height, _ = keep_ref.shape
        width = parts * strip
        latw = glat_s.shape[1]
        for g in range(G):
            own = slice(g * wide, (g + 1) * wide)
            for j in range(each):
                cols = slice(j * strip, (j + 1) * strip)
                gku_s[own, cols] = nn(latt_ref[own, :], gk_refs[g * each + j][...])
                gvu_s[own, cols] = nn(latt_ref[own, :], gv_refs[g * each + j][...])
        d = gn_s.shape[1]
        norm_in = jnp.broadcast_to(gn_s[0:1, :], (PAIR, d)).astype(BF16)
        norm_mid = jnp.broadcast_to(gn_mid_ref[0:1, :], (PAIR, d)).astype(BF16)
        gn_cols = (norm_in.T, norm_mid.T)
        own_rows = 2 * up_rows
        owners = height // own_rows
        core = core_ref[0]
        for p in range(pairs):
            for mine, ref in ((False, send_ref), (True, keep_ref)):
                which = 2 * p + (core if mine else 1 - core)
                at = pl.ds(pl.multiple_of(which * height, height), height)
                m = nt_ref[at, :]
                for part in range(parts):
                    cols = slice(part * strip, (part + 1) * strip)
                    ref[0, p, :, cols] = nn(m, gq_refs[part][...]).astype(BF16)
                ref[1, p, :, 0:latw] = nn(m, glat_s[...]).astype(BF16)
                near = pl.ds(pl.multiple_of(which * (height // 2), height // 2), height // 2)
                keys, values = gku_s[near, :], gvu_s[near, :]
                if up_rows % 8:
                    ups = nn(interleave(up_rows, height), jnp.concatenate([keys, values], axis=0).astype(BF16))
                else:
                    pieces = []
                    for j in range(owners):
                        pieces.append(keys[j * up_rows : (j + 1) * up_rows])
                        pieces.append(values[j * up_rows : (j + 1) * up_rows])
                    ups = jnp.concatenate(pieces, axis=0)
                ref[1, p, :, latw : latw + out] = ups.astype(BF16)
                for h in range(2):
                    a, b = (gn_cols[h][(2 * p + c) * height :][:height] for c in range(2))
                    flip = (core == 0) if mine else (core == 1)
                    ref[h, p, :, width:] = jnp.where(flip, a, b)


def project_back(core, gq, gk, gv, latt, nt_, tokens, ghid, first, ku, vu, gains, gn_mid, n_dp, up_rows):
    count, d = tokens.shape
    parts = len(gq)
    width = sum(x.shape[1] for x in gq)
    latw = latt.shape[0]
    height = d // n_dp
    tile = lambda wide: pl.BlockSpec((TILE, wide), lambda i, *_: (i, 0))
    grads = (2, n_dp // 2, height, width + PAIR)
    return pl.pallas_call(
        functools.partial(project_back_kernel, up_rows),
        grid_spec=pltpu.PrefetchScalarGridSpec(
            num_scalar_prefetch=1,
            grid=(count // TILE,),
            in_specs=[whole(x.shape) for x in (*gq, *gk, *gv)]
            + [
                whole((latw, count)),
                whole((d, count)),
                tile(d),
                tile(d),
                pl.BlockSpec((d, width), lambda i, *_: (0, 0)),
                pl.BlockSpec((d, latw), lambda i, *_: (0, (width + d) // latw)),
                whole(ku.shape),
                whole(vu.shape),
                whole((8, d)),
                whole((8, d)),
            ],
            out_specs=[tile(d), whole(grads), whole(grads)],
            scratch_shapes=[
                pltpu.VMEM((count, latw), BF16),
                pltpu.VMEM((8, d), F32),
                pltpu.VMEM(ku.shape, F32),
                pltpu.VMEM(vu.shape, F32),
            ],
        ),
        out_shape=[shape_of((count, d), BF16), shape_of(grads, BF16), shape_of(grads, BF16)],
        cost_estimate=cost(17),
        compiler_params=params(),
        name="project_back",
    )(core, *gq, *gk, *gv, latt, nt_, tokens, ghid, first, first, ku, vu, gains, gn_mid)


def swap(values, axis_name, bit):
    size = lax.axis_size(axis_name)
    return lax.ppermute(values, axis_name, [(i, i ^ bit) for i in range(size)])


def bits_of(axis_name):
    size = lax.axis_size(axis_name)
    return [1 << i for i in range(size.bit_length() - 1)]


def owner_bits():
    names = [("dp", bit) for bit in reversed(bits_of("dp")) if bit > 1]
    return names + [("fsdp", bit) for bit in reversed(bits_of("fsdp"))]


def add(a, b, dtype=BF16):
    return (a.astype(F32) + b.astype(F32)).astype(dtype)


def part_of(values, names, which, mine, trail=2):
    axis_name, bit = which
    own = (lax.axis_index(axis_name) // bit) % 2
    at = values.ndim - trail - len(names) + names.index(which)
    return lax.dynamic_index_in_dim(values, own if mine else 1 - own, at, keepdims=False)


def scatter_rounds(keep, send):
    (came,) = yield [(send, "dp", 1)]
    names = owner_bits()
    rows = keep.size // (2 * keep.shape[-1]) >> len(names)
    shape = (2,) * len(names) + (rows, keep.shape[-1])
    keep, came = keep.reshape((2,) + shape), came.reshape((2,) + shape)
    firsts = [("fsdp", 1), ("dp", 2)]
    parts = [(keep[0], came[0]), (keep[1], came[1])]
    left = [names, names]
    for orders in (firsts, firsts[::-1]):
        split = [
            [add(*(part_of(x, kept, which, mine) for x in part)) for mine in (False, True)]
            for part, kept, which in zip(parts, left, orders)
        ]
        come = yield [(send, *which) for (send, _), which in zip(split, orders)]
        parts = [(keep, here) for (_, keep), here in zip(split, come)]
        left = [
            [name for name in kept if name != which] for kept, which in zip(left, orders)
        ]
    both, names = jnp.stack([add(*part) for part in parts]), left[0]
    rest = sorted(names, key=lambda name: (name[0] != "fsdp", name[1]))
    for which in rest:
        (came,) = yield [(part_of(both, names, which, False), *which)]
        both = add(
            part_of(both, names, which, True), came, F32 if which == rest[-1] else BF16
        )
        names = [name for name in names if name != which]
    return both


def gather_rounds(values):
    names = owner_bits()
    firsts = [("fsdp", 1), ("dp", 2)]
    rest = [name for name in names if name not in firsts]
    rest = sorted(rest, key=lambda name: (name[0] != "fsdp", name[1]), reverse=True)
    every = [("dp", 1 << i) for i in reversed(range(len(bits_of("dp"))))]
    every += [("fsdp", 1 << i) for i in reversed(range(len(bits_of("fsdp"))))]

    def join(part, came, have, which):
        have = sorted(have + [which], key=every.index)
        axis_name, bit = which
        low = (lax.axis_index(axis_name) // bit) % 2 == 0
        pair = (jnp.where(low, part, came), jnp.where(low, came, part))
        return jnp.stack(pair, axis=have.index(which)), have

    have = []
    for which in rest:
        (came,) = yield [(values, *which)]
        values, have = join(values, came, have, which)
    cut = values.shape[-1] // 256 * 128
    parts = [values[..., :cut], values[..., cut:]]
    haves = [have, have]
    for orders in (firsts, firsts[::-1], [("dp", 1)] * 2):
        come = yield [(part, *which) for part, which in zip(parts, orders)]
        both = [join(*item) for item in zip(parts, come, haves, orders)]
        parts, haves = [x[0] for x in both], [x[1] for x in both]
    whole_ = jnp.concatenate(parts, axis=-1)
    return whole_.reshape(-1, whole_.shape[-1])


class Rounds:
    def __init__(self, steps):
        self.steps = steps
        self.wants = next(self.steps)
        self.done = None

    def after(self, other):
        values = [want[0] for want in self.wants]
        values, _ = lax.optimization_barrier((values, [want[0] for want in other.wants]))
        self.wants = [(value, *want[1:]) for value, want in zip(values, self.wants)]

    def take(self, come):
        try:
            self.wants = self.steps.send(come)
        except StopIteration as end:
            self.wants, self.done = [], end.value


def beside(held, runs, work):
    sends = [[want[0] for want in run.wants] for run in runs]
    held, sends = lax.optimization_barrier((held, sends))
    come = [
        [swap(values, *want[1:]) for values, want in zip(group, run.wants)]
        for group, run in zip(sends, runs)
    ]
    result = work(held)
    result, come = lax.optimization_barrier((result, come))
    for run, here in zip(runs, come):
        run.take(here)
    return result


def together(runs):
    beside((), runs, lambda held: held)


def finish(runs):
    while any(run.wants for run in runs):
        live = [run for run in runs if run.wants]
        come = [[swap(*want) for want in run.wants] for run in live]
        for run, here in zip(live, come):
            run.take(here)


def shards(
    tokens,
    doc_ids,
    norm_in,
    query_weight,
    latent_weight,
    key_up_weight,
    value_up_weight,
    output_weight,
    norm_mid,
    gate_weight,
    up_weight,
    down_weight,
    cotangent,
):
    both = ("dp", "fsdp")
    n_dp = lax.axis_size("dp")
    devices = n_dp * lax.axis_size("fsdp")
    own_rows, d = query_weight.shape
    d_all = own_rows * devices
    latw = latent_weight.shape[1]
    up_rows, up_width = key_up_weight.shape
    ff = gate_weight.shape[1]

    gains = jnp.stack([norm_in, norm_mid], axis=1)
    gains = jnp.pad(gains, ((0, 0), (0, PAIR - 2)))
    packed = jnp.concatenate(
        [
            query_weight,
            output_weight,
            latent_weight,
            jnp.concatenate([key_up_weight, value_up_weight], axis=0),
            gains,
        ],
        axis=1,
    )
    steps = ff // TILE
    cut = (steps + 1) // 2
    down_rows = down_weight.shape[0]
    folds = -(-down_rows // own_rows)
    down_own = jnp.pad(down_weight, ((0, folds * own_rows - down_rows), (0, 0)))
    wide = jnp.concatenate(
        [down_own[i * own_rows : (i + 1) * own_rows] for i in range(folds)]
        + [gate_weight, up_weight],
        axis=1,
    )
    gate_at = folds * d // TILE
    get_first = Rounds(gather_rounds(packed))
    for _ in range(0):
        together([get_first])
    wide = beside(wide, [get_first], lambda held: held)
    wide = lax.all_gather(wide, both, axis=0, tiled=True)
    while get_first.wants:
        together([get_first])
    first = get_first.done

    at = 2 * d + latw
    ups = first[:, at : at + up_width].reshape(devices, 2, up_rows, up_width)
    ku = ups[:, 0].reshape(devices * up_rows, up_width)
    vu = ups[:, 1].reshape(devices * up_rows, up_width)
    mask = visible(doc_ids)
    core = (lax.axis_index("dp") % 2).astype(jnp.int32).reshape(1)

    q, lat, latt, k, v, normed_t, gain_rows = project(tokens, first, ku, vu)
    pairs = q.shape[1] // PAIR
    halves = [attend(mask, q, k, v, 0, pairs)]
    wo = (first, pl.BlockSpec((d_all, d), lambda i, *_: (0, 1)))
    hid, mid, midt = middle([half[0] for half in halves], wo, tokens, gain_rows)
    down = unfold(wide, own_rows, down_rows, d)
    out, gmid, keep_a, send_a, gdown = feed(
        core, mid, midt, cotangent, hid, None, (wide, gate_at), (wide, gate_at + steps), down, (0, cut), 0, n_dp, ff
    )
    lead = d // 2
    run_a = Rounds(scatter_rounds(keep_a, send_a))
    layer_out, gmid, keep_b, send_b, gdown = beside(
        out,
        [run_a],
        lambda out: feed(
            core,
            mid,
            midt,
            cotangent,
            out,
            (gmid, gdown),
            (wide, gate_at),
            (wide, gate_at + steps),
            down,
            (cut, steps),
            lead,
            n_dp,
            ff,
        ),
    )
    split = gdown.reshape(2, n_dp // 2, 2, ff // n_dp, d // 2)
    run_d = Rounds(
        scatter_rounds(
            lax.dynamic_index_in_dim(split, core[0], 2, keepdims=False),
            lax.dynamic_index_in_dim(split, 1 - core[0], 2, keepdims=False),
        )
    )
    ghid, gatt, keep_b, send_b, gnorm_mid = beside(
        gmid,
        [run_a, run_d],
        lambda gmid: middle_back(
            core,
            gmid,
            hid,
            cotangent,
            [half[1] for half in halves],
            wo,
            gain_rows,
            keep_b,
            send_b,
        ),
    )
    run_b = Rounds(scatter_rounds(keep_b, send_b))
    gq, gk, gv = [], [], []
    plan = ([run_a, run_b], [run_d, run_a], [run_b, run_a], [run_b, run_d])
    each = pairs // len(plan)
    for part, runs in enumerate(plan):
        half = halves[part * len(halves) // len(plan)]
        at = part * each % (pairs // len(halves))
        pieces = beside(
            gatt,
            runs,
            lambda gatt: attend_back(
                mask, q, k, v, half[0], gatt, half[2], part * each, at, each
            ),
        )
        for kept, piece in zip((gq, gk, gv), pieces):
            kept.append(piece)
    gtok, keep_c, send_c = beside(
        ghid,
        [run_b, run_d],
        lambda ghid: project_back(
            core,
            gq,
            gk,
            gv,
            latt,
            normed_t,
            tokens,
            ghid,
            first,
            ku,
            vu,
            gain_rows,
            gnorm_mid,
            n_dp,
            up_rows,
        ),
    )
    run_c = Rounds(scatter_rounds(keep_c, send_c))
    last = [run_b, run_d]
    come = [[swap(*want) for want in run.wants] for run in last]
    for _ in range(3):
        together([run_c])
    kept, come = lax.optimization_barrier(([want[0] for want in run_c.wants], come))
    run_c.wants = [(value, *want[1:]) for value, want in zip(kept, run_c.wants)]
    finish([run_c])
    for run, here in zip(last, come):
        run.take(here)
    finish([run_a, run_b, run_d])
    s_a, s_b, s_c, s_down = (run.done for run in (run_a, run_b, run_c, run_d))
    merge = lambda a, b: jnp.concatenate([a, b], axis=1)
    return (
        layer_out,
        gtok,
        s_c[0, :, d],
        s_c[0, :, :d],
        s_c[1, :, :latw],
        s_c[1, :up_rows, latw : latw + up_width],
        s_c[1, up_rows:, latw : latw + up_width],
        merge(s_b[0, :, :lead], s_b[1, :, :lead]),
        s_c[1, :, d],
        merge(s_a[0], s_b[0, :, lead:]),
        merge(s_a[1], s_b[1, :, lead:]),
        merge(s_down[0], s_down[1]),
    )


def solution(mesh):
    split = ("dp", "fsdp")
    flat, matrix = P(split), P(split, None)
    return jax.shard_map(
        shards,
        mesh=mesh,
        in_specs=(
            matrix,
            matrix,
            flat,
            matrix,
            matrix,
            matrix,
            matrix,
            matrix,
            flat,
            matrix,
            matrix,
            matrix,
            matrix,
        ),
        out_specs=(
            matrix,
            matrix,
            flat,
            matrix,
            matrix,
            matrix,
            matrix,
            matrix,
            flat,
            matrix,
            matrix,
            matrix,
        ),
        check_vma=False,
    )
```

time: 624 us -> 477 us (0.76)
  waiting for transfers between devices: 275 us -> 156 us
  Pallas kernels: 209 us -> 190 us
  other arithmetic: 45.6 us -> 37.8 us
  local copies, waits for them, and re-layouts: 31.5 us -> 38.5 us
    all_gather x3 -> x1, waiting for transfers between devices: 181 us -> 27.2 us  [shards(): wide = lax.all_gather(wide, both, axis=0, tiled=True)]
    ppermute x36, waiting for transfers between devices: 93.9 us -> 129 us  [swap(): return lax.ppermute(values, axis_name, [(i, i ^ bit) for i in range(size)])]
    concatenate x4 -> x5, other arithmetic: 22.6 us -> 3.83 us  [the longest x4 2.94 us: shards(): merge = lambda a, b: jnp.concatenate([a, b], axis=1)]
    pallas_call x1, Pallas kernels: 33.5 us -> 19.4 us  [attend(): pl.pallas_call(attend_kernel, grid_spec=pltpu.PrefetchScalarGridSpec(num_...]
    another operation x1 -> x23, other arithmetic: 0.01 us -> 9.81 us  [the longest x8 7.69 us: scatter_rounds(): both, names = (jnp.stack([add(*part) for part in parts]), left[0])]
    dynamic_slice x7 -> x14, local copies, waits for them, and re-layouts: 16.3 us -> 7.7 us  [part_of(): lax.dynamic_index_in_dim(values, own if mine else 1 - own, at, keepdims=F...]
    unnamed x18 -> x72, local copies, waits for them, and re-layouts: 6.49 us -> 14.4 us
    pallas_call x1 -> x4, Pallas kernels: 40.7 us -> 35.3 us  [attend_back(): pl.pallas_call(attend_back_kernel, grid_spec=pltpu.PrefetchScalarGridSpec...]
  transfers between devices with their start and end apart: 39 -> 37, of which waited for: 26 -> 25; matrix products, arithmetic and copies ran while one was open for 10% -> 8% of each run, Pallas kernels for 8% -> 28%
where the time goes in v2:
time: 477 us; the launch traced here: 472 us
  Pallas kernels  190 us (40%)
  waiting for transfers between devices  156 us (33%)
  local copies, waits for them, and re-layouts  38.5 us (8%)
  other arithmetic  37.8 us (8%)
  starting transfers between devices  35.1 us (7%)
  between operations  15.2 us (3%)
    ppermute x36, waiting for transfers between devices, swap(): return lax.ppermute(values, axis_name, [(i, i ^ bit) for i in range(size)])  129 us
    pallas_call x2, Pallas kernels, feed(): pl.pallas_call(functools.partial(feed_kernel, first, last), grid_spec=plt...  76.9 us
    pallas_call x4, Pallas kernels, attend_back(): pl.pallas_call(attend_back_kernel, grid_spec=pltpu.PrefetchScalarGridSpec...  35.3 us
    ppermute x36, starting transfers between devices, swap(): return lax.ppermute(values, axis_name, [(i, i ^ bit) for i in range(size)])  35.1 us
    all_gather x1, waiting for transfers between devices, shards(): wide = lax.all_gather(wide, both, axis=0, tiled=True)  27.2 us
    pallas_call x1, Pallas kernels, project_back(): pl.pallas_call(functools.partial(project_back_kernel, up_rows), grid_spec...  20.8 us
    convert_element_type x28, other arithmetic, add(): return (a.astype(F32) + b.astype(F32)).astype(dtype)  19.7 us
    pallas_call x1, Pallas kernels, attend(): pl.pallas_call(attend_kernel, grid_spec=pltpu.PrefetchScalarGridSpec(num_...  19.4 us
  transfers between devices with their start and end apart: 37, of which 25 were waited for; matrix products, arithmetic and copies ran while one was open for 8% of the time, Pallas kernels for 28%

profile of v2, /device:TPU:0, one launch (start us, length us, event | category | flops | bytes accessed | tf_op | source)
XLA Modules:
  0.0 472.2 jit_solution(1402381657771120829)
XLA Ops:
  19.7 9.5 %collective-permute-done = bf16[32,3200]{1,0:T(8,128)(2,1)S(1)} collective-permute-done((bf16[32,3200]{1,0:T(8,128)(2,1)S(1)}, bf16[32,3200]{1,0:T(8,128)(2,1)S(1)}, u32[]{:S(2)}, u32[]{:S(2)}) %collective-permute-start) | collective-permute-done | bytes 204832 | tf_op jit(solution)/shard_map/ppermute | solution.py:736
  30.2 9.9 %collective-permute-done.1 = bf16[2,32,3200]{2,1,0:T(8,128)(2,1)S(1)} collective-permute-done((bf16[2,32,3200]{2,1,0:T(8,128)(2,1)S(1)}, bf16[2,32,3200]{2,1,0:T(8,128)(2,1)S(1)}, u32[]{:S(2)}, u32[]{:S(2)}) %collective-permute-start.1) | collective-permute-done | bytes 409632 | tf_op jit(solution)/shard_map/ppermute | solution.py:736
  43.2 11.1 %collective-permute-done.2 = bf16[2,2,32,1536]{3,2,0,1:T(8,128)(2,1)S(1)} collective-permute-done((bf16[2,2,32,1536]{3,2,0,1:T(8,128)(2,1)S(1)}, bf16[2,2,32,1536]{3,2,0,1:T(8,128)(2,1)S(1)}, u32[]{:S(2)}, u32[]{:S(2)}) %collective-permute-start.2) | collective-permute-done | bytes 393248 | tf_op jit(solution)/shard_map/ppermute | solution.py:736
  58.0 24.5 %collective-permute-done.4 = bf16[2,2,2,32,1536]{4,3,0,1,2:T(8,128)(2,1)S(1)} collective-permute-done((bf16[2,2,2,32,1536]{4,3,0,1,2:T(8,128)(2,1)S(1)}, bf16[2,2,2,32,1536]{4,3,0,1,2:T(8,128)(2,1)S(1)}, u32[]{:S(2)}, u32[]{:S(2)}) %collective-permute-start.4) | collective-permute-done | bytes 786464 | tf_op jit(solution)/shard_map/ppermute | solution.py:736
  82.5 4.9 %collective-permute-done.5 = bf16[2,2,2,32,1664]{4,3,1,2,0:T(8,128)(2,1)S(1)} collective-permute-done((bf16[2,2,2,32,1664]{4,3,1,2,0:T(8,128)(2,1)S(1)}, bf16[2,2,2,32,1664]{4,3,1,2,0:T(8,128)(2,1)S(1)}, u32[]{:S(2)}, u32[]{:S(2)}) %collective-permute-start.5) | collective-permute-done | bytes 852000 | tf_op jit(solution)/shard_map/ppermute | solution.py:736
  100.1 9.5 %project.1 = (bf16[1024,1024]{1,0:T(8,128)(2,1)}, bf16[1024,512]{1,0:T(8,128)(2,1)}, bf16[512,1024]{1,0:T(8,128)(2,1)}, bf16[1024,1024]{1,0:T(8,128)(2,1)}, bf16...) custom-call(bf16[1024,1024]{1,0:T(8,128)(2,1)} %refs_14_.1, bf16[1024,3200]{1,0:T(8,128)(2,1)} %bitcast.316, ...), custom_call_target="tpu_custom_call" | custom-call | flops 11000000512 | tf_op jit(solution)/shard_map/project/pallas_call | solution.py:107
  109.5 19.4 %attend.1 = (bf16[1024,1024]{1,0:T(8,128)(2,1)}, bf16[1024,1024]{1,0:T(8,128)(2,1)}, f32[8,8,1024]{2,1,0:T(8,128)}) custom-call(bf16[1024,1024]{1,0:T(8,128)(2,1)} %get-tuple-element.166.q_ref, bf16[1024,1024]{1,0:T(8,128)(2,1)} %get-tuple-element.167.k_ref, bf16[1024,1024]{1,0:T(8,128)(2,1)} %get-tuple-element.168.v_ref, bf16[8,640,128]{2,1,0:T(8,128)(2,1)} %copy-done.29), custom_call_target="tpu_custom_call" | custom-call | flops 22000001024 | tf_op jit(solution)/shard_map/attend/pallas_call | solution.py:195
  128.9 8.1 %middle.1 = (f32[1024,1024]{1,0:T(8,128)}, bf16[1024,1024]{1,0:T(8,128)(2,1)}, bf16[1024,1024]{1,0:T(8,128)(2,1)}) custom-call(bf16[1024,1024]{1,0:T(8,128)(2,1)} %get-tuple-element.169.refs_0_.o_ref, bf16[1024,3200]{1,0:T(8,128)(2,1)} %bitcast.319, bf16[1024,1024]{1,0:T(8,128)(2,1)} %refs_14_.1, f32[8,1024]{1,0:T(8,128)} %get-tuple-element.170.refs_3_.refs_2_.refs_20_), custom_call_target="tpu_custom_call" | custom-call | flops 8800000000 | tf_op jit(solution)/shard_map/middle/pallas_call | solution.py:318
  137.0 27.2 %all-gather.2.cloned.1.call-done.in_ref.refs_4_.refs_5_.refs_6_.refs_7_ = bf16[1024,8704]{1,0:T(8,128)(2,1)} async-done(((bf16[32,8704]{1,0:T(8,128)(2,1)}), bf16[1024,8704]{1,0:T(8,128)(2,1)}) %all-gather.2.cloned.1.call-update) | async-done | bytes 17825808 | tf_op jit(solution)/shard_map/all_gather | solution.py:915
  164.2 5.8 %unfold.1.refs_6_.refs_8_ = bf16[2816,1024]{1,0:T(8,128)(2,1)} custom-call(bf16[1024,8704]{1,0:T(8,128)(2,1)} %all-gather.2.cloned.1.call-done.in_ref.refs_4_.refs_5_.refs_6_.refs_7_), custom_call_target="tpu_custom_call" | custom-call | flops 5500000256 | tf_op jit(solution)/shard_map/unfold/pallas_call | solution.py:353
  169.9 41.0 %feed.2 = (f32[1024,1024]{1,0:T(8,128)}, f32[1024,1024]{1,0:T(8,128)}, bf16[2,2,256,1536]{3,2,1,0:T(8,128)(2,1)}, bf16[2,2,256,1536]{3,2,1,0:T(8,128)(2,1)}, bf16[2,2816,512]{2,1,0:T(8,128)(2,1)}) custom-call(s32[1]{0:T(128)} %bitcast.core_ref, bf16[1024,1024]{1,0:T(8,128)(2,1)} %get-tuple-element.171.refs_0_, ...), custom_call_target="tpu_custom_call" | custom-call | flops 49500000256 | tf_op jit(solution)/shard_map/feed/pallas_call | solution.py:449
  215.6 35.9 %feed.3 = (bf16[1024,1024]{1,0:T(8,128)(2,1)}, f32[1024,1024]{1,0:T(8,128)}, bf16[2,2,256,1792]{3,2,1,0:T(8,128)(2,1)}, bf16[2,2,256,1792]{3,2,1,0:T(8,128)(2,1)}, bf16[2,2816,512]{2,1,0:T(8,128)(2,1)}) custom-call(s32[1]{0:T(128)} %bitcast.core_ref, bf16[1024,1024]{1,0:T(8,128)(2,1)} %get-tuple-element.171.refs_0_, ...), custom_call_target="tpu_custom_call", output_to_operand_aliasing={{4}: (6, {})} | custom-call | flops 41250000896 | tf_op jit(solution)/shard_map/feed/pallas_call | solution.py:449
  259.2 14.0 %middle_back.1 = (f32[1024,1024]{1,0:T(8,128)}, bf16[1024,1024]{1,0:T(8,128)(2,1)}, bf16[2,2,256,1792]{3,2,1,0:T(8,128)(2,1)}, bf16[2,2,256,1792]{3,2,1,0:T(8,128)(2,1)}, f32[8,1024]{1,0:T(8,128)}) custom-call(s32[1]{0:T(128)} %bitcast.core_ref, f32[1024,1024]{1,0:T(8,128)} %get-tuple-element.191.gmid_ref, ...), custom_call_target="tpu_custom_call", output_to_operand_aliasing={{2}: (7, {}), {3}: (8, {})} | custom-call | flops 13200000000 | tf_op jit(solution)/shard_map/middle_back/pallas_call | solution.py:545
  293.5 8.7 %attend_back.4 = (bf16[1024,256]{1,0:T(8,128)(2,1)}, bf16[1024,256]{1,0:T(8,128)(2,1)}, bf16[1024,256]{1,0:T(8,128)(2,1)}) custom-call(bf16[1024,1024]{1,0:T(8,128)(2,1)} %get-tuple-element.166.q_ref, bf16[1024,1024]{1,0:T(8,128)(2,1)} %get-tuple-element.167.k_ref, bf16[1024,1024]{1,0:T(8,128)(2,1)} %get-tuple-element.168.v_ref, ...), custom_call_target="tpu_custom_call" | custom-call | flops 7699999744 | tf_op jit(solution)/shard_map/attend_back/pallas_call | solution.py:277
  308.0 8.9 %attend_back.5 = (bf16[1024,256]{1,0:T(8,128)(2,1)}, bf16[1024,256]{1,0:T(8,128)(2,1)}, bf16[1024,256]{1,0:T(8,128)(2,1)}) custom-call(bf16[1024,1024]{1,0:T(8,128)(2,1)} %get-tuple-element.166.q_ref, bf16[1024,1024]{1,0:T(8,128)(2,1)} %get-tuple-element.167.k_ref, bf16[1024,1024]{1,0:T(8,128)(2,1)} %get-tuple-element.168.v_ref, ...), custom_call_target="tpu_custom_call" | custom-call | flops 7699999744 | tf_op jit(solution)/shard_map/attend_back/pallas_call | solution.py:277
  329.5 5.5 %collective-permute-done.15 = bf16[2,2,2,88,512]{4,3,2,1,0:T(8,128)(2,1)S(1)} collective-permute-done((bf16[2,2,2,88,512]{4,3,2,1,0:T(8,128)(2,1)}, bf16[2,2,2,88,512]{4,3,2,1,0:T(8,128)(2,1)S(1)}, u32[]{:S(2)}, u32[]{:S(2)}) %collective-permute-start.15) | collective-permute-done | bytes 720928 | tf_op jit(solution)/shard_map/ppermute | solution.py:736
  339.8 8.7 %attend_back.6 = (bf16[1024,256]{1,0:T(8,128)(2,1)}, bf16[1024,256]{1,0:T(8,128)(2,1)}, bf16[1024,256]{1,0:T(8,128)(2,1)}) custom-call(bf16[1024,1024]{1,0:T(8,128)(2,1)} %get-tuple-element.166.q_ref, bf16[1024,1024]{1,0:T(8,128)(2,1)} %get-tuple-element.167.k_ref, bf16[1024,1024]{1,0:T(8,128)(2,1)} %get-tuple-element.168.v_ref, ...), custom_call_target="tpu_custom_call" | custom-call | flops 7699999744 | tf_op jit(solution)/shard_map/attend_back/pallas_call | solution.py:277
  352.2 5.7 %collective-permute-done.18 = bf16[2,2,2,32,1792]{4,3,1,2,0:T(8,128)(2,1)} collective-permute-done((bf16[2,2,2,32,1792]{4,3,1,2,0:T(8,128)(2,1)}, bf16[2,2,2,32,1792]{4,3,1,2,0:T(8,128)(2,1)}, u32[]{:S(2)}, u32[]{:S(2)}) %collective-permute-start.18) | collective-permute-done | bytes 917536 | tf_op jit(solution)/shard_map/ppermute | solution.py:736
  365.2 9.1 %attend_back.7 = (bf16[1024,256]{1,0:T(8,128)(2,1)}, bf16[1024,256]{1,0:T(8,128)(2,1)}, bf16[1024,256]{1,0:T(8,128)(2,1)}) custom-call(bf16[1024,1024]{1,0:T(8,128)(2,1)} %get-tuple-element.166.q_ref, bf16[1024,1024]{1,0:T(8,128)(2,1)} %get-tuple-element.167.k_ref, bf16[1024,1024]{1,0:T(8,128)(2,1)} %get-tuple-element.168.v_ref, ...), custom_call_target="tpu_custom_call" | custom-call | flops 7699999744 | tf_op jit(solution)/shard_map/attend_back/pallas_call | solution.py:277
  374.3 4.7 collective-permute-done.23
  387.2 20.8 %project_back.1 = (bf16[1024,1024]{1,0:T(8,128)(2,1)}, bf16[2,2,256,1152]{3,2,1,0:T(8,128)(2,1)}, bf16[2,2,256,1152]{3,2,1,0:T(8,128)(2,1)}) custom-call(s32[1]{0:T(128)} %bitcast.core_ref, bf16[1024,256]{1,0:T(8,128)(2,1)} %get-tuple-element.215.refs_0_, bf16[1024,256]{1,0:T(8,128)(2,1)} %get-tuple-element.226.refs_1_, ...), custom_call_target="tpu_custom_call" | custom-call | flops 18699999232 | tf_op jit(solution)/shard_map/project_back/pallas_call | solution.py:701
  416.6 13.1 %collective-permute-done.28 = bf16[2,2,2,32,1152]{4,3,1,2,0:T(8,128)(2,1)S(1)} collective-permute-done((bf16[2,2,2,32,1152]{4,3,1,2,0:T(8,128)(2,1)S(1)}, bf16[2,2,2,32,1152]{4,3,1,2,0:T(8,128)(2,1)S(1)}, u32[]{:S(2)}, u32[]{:S(2)}) %collective-permute-start.28) | collective-permute-done | bytes 589856 | tf_op jit(solution)/shard_map/ppermute | solution.py:736
  446.0 7.4 %collective-permute-done.34 = bf16[2,2,32,1152]{3,2,0,1:T(8,128)(2,1)S(1)} collective-permute-done((bf16[2,2,32,1152]{3,2,0,1:T(8,128)(2,1)S(1)}, bf16[2,2,32,1152]{3,2,0,1:T(8,128)(2,1)S(1)}, u32[]{:S(2)}, u32[]{:S(2)}) %collective-permute-start.34) | collective-permute-done | bytes 294944 | tf_op jit(solution)/shard_map/ppermute | solution.py:736
  455.0 7.5 %collective-permute-done.35 = bf16[2,32,1152]{2,1,0:T(8,128)(2,1)S(1)} collective-permute-done((bf16[2,32,1152]{2,1,0:T(8,128)(2,1)S(1)}, bf16[2,32,1152]{2,1,0:T(8,128)(2,1)S(1)}, u32[]{:S(2)}, u32[]{:S(2)}) %collective-permute-start.35) | collective-permute-done | bytes 147488 | tf_op jit(solution)/shard_map/ppermute | solution.py:736
  (266 shorter events, 136.3 us)
Async XLA Ops:
  7.2 157.0 %all-gather.2.cloned.1.call-start = ((), (), s32[]{:S(2)}) async-start(), calls=%async_computation | async-start | bytes 18382848 | tf_op jit(solution)/shard_map/all_gather | solution.py:915
  40.3 14.1 %collective-permute-start.3 = (bf16[2,2,32,1664]{3,2,0,1:T(8,128)(2,1)S(1)}, bf16[2,2,32,1664]{3,2,0,1:T(8,128)(2,1)S(1)}, u32[]{:S(2)}, u32[]{:S(2)}) collective-permute-start(bf16[2,2,32,1664]{3,2,0,1:T(8,128)(2,1)S(1)} %pad_maximum_fusion.4), channel_id=1, source_target_pairs={{0,16},{8,24},{16,0},{24,8},{1,17},{9,25},{17,1},{25,9},{2,18},{10... | collective-permute-start | bytes 1277960 | tf_op jit(solution)/shard_map/ppermute | solution.py:736
  54.9 32.4 %collective-permute-start.5 = (bf16[2,2,2,32,1664]{4,3,1,2,0:T(8,128)(2,1)S(1)}, bf16[2,2,2,32,1664]{4,3,1,2,0:T(8,128)(2,1)S(1)}, u32[]{:S(2)}, u32[]{:S(2)}) collective-permute-start(bf16[2,2,2,32,1664]{4,3,1,2,0:T(8,128)(2,1)S(1)} %pad_maximum_fusion.2), channel_id=1, source_target_pairs={{0,1},{1,0},{2,3},{3,2},{4,5},{5,4},{6,7},{7,6},{8,9},{9,8},{10,11... | collective-permute-start | bytes 2555912 | tf_op jit(solution)/shard_map/ppermute | solution.py:736
  56.3 26.2 %collective-permute-start.4 = (bf16[2,2,2,32,1536]{4,3,0,1,2:T(8,128)(2,1)S(1)}, bf16[2,2,2,32,1536]{4,3,0,1,2:T(8,128)(2,1)S(1)}, u32[]{:S(2)}, u32[]{:S(2)}) collective-permute-start(bf16[2,2,2,32,1536]{4,3,0,1,2:T(8,128)(2,1)S(1)} %pad_maximum_fusion.3), channel_id=1, source_target_pairs={{0,16},{8,24},{16,0},{24,8},{1,17},{9,25},{17,1},{25,9},{2,18},{10... | collective-permute-start | bytes 2359304 | tf_op jit(solution)/shard_map/ppermute | solution.py:736
  210.9 40.6 %collective-permute-start.8 = (bf16[2,2,256,1536]{3,2,1,0:T(8,128)(2,1)}, bf16[2,2,256,1536]{3,2,1,0:T(8,128)(2,1)S(1)}, u32[]{:S(2)}, u32[]{:S(2)}) collective-permute-start(bf16[2,2,256,1536]{3,2,1,0:T(8,128)(2,1)} %get-tuple-element.185), channel_id=1, source_target_pairs={{0,8},{8,0},{16,24},{24,16},{1,9},{9,1},{17,25},{25,17},{2,10},{10... | collective-permute-start | bytes 9437192 | tf_op jit(solution)/shard_map/ppermute | solution.py:736
  256.9 21.4 %collective-permute-start.11 = (bf16[2,2,704,512]{3,2,1,0:T(8,128)(2,1)}, bf16[2,2,704,512]{3,2,1,0:T(8,128)(2,1)}, u32[]{:S(2)}, u32[]{:S(2)}) collective-permute-start(bf16[2,2,704,512]{3,2,1,0:T(8,128)(2,1)} %dynamic-slice_bitcast_fusion), channel_id=1, source_target_pairs={{0,8},{8,0},{16,24},{24,16},{1,9},{9,1},{17,25},{25,17},{2,10},{10... | collective-permute-start | bytes 8650760 | tf_op jit(solution)/shard_map/ppermute | solution.py:736
  257.2 19.9 %collective-permute-start.10 = (bf16[2,2,2,32,1536]{4,3,0,1,2:T(8,128)(2,1)}, bf16[2,2,2,32,1536]{4,3,0,1,2:T(8,128)(2,1)S(1)}, u32[]{:S(2)}, u32[]{:S(2)}) collective-permute-start(bf16[2,2,2,32,1536]{4,3,0,1,2:T(8,128)(2,1)} %fusion.10), channel_id=1, source_target_pairs={{0,16},{8,24},{16,0},{24,8},{1,17},{9,25},{17,1},{25,9},{2,18},{10... | collective-permute-start | bytes 2359304 | tf_op jit(solution)/shard_map/ppermute | solution.py:736
  258.7 19.6 %collective-permute-start.9 = (bf16[2,2,2,32,1536]{4,3,1,2,0:T(8,128)(2,1)}, bf16[2,2,2,32,1536]{4,3,1,2,0:T(8,128)(2,1)S(1)}, u32[]{:S(2)}, u32[]{:S(2)}) collective-permute-start(bf16[2,2,2,32,1536]{4,3,1,2,0:T(8,128)(2,1)} %fusion.9), channel_id=1, source_target_pairs={{0,1},{1,0},{2,3},{3,2},{4,5},{5,4},{6,7},{7,6},{8,9},{9,8},{10,11... | collective-permute-start | bytes 2359304 | tf_op jit(solution)/shard_map/ppermute | solution.py:736
  280.1 24.7 %collective-permute-start.14 = (bf16[2,2,256,1792]{3,2,1,0:T(8,128)(2,1)}, bf16[2,2,256,1792]{3,2,1,0:T(8,128)(2,1)}, u32[]{:S(2)}, u32[]{:S(2)}) collective-permute-start(bf16[2,2,256,1792]{3,2,1,0:T(8,128)(2,1)} %get-tuple-element.214), channel_id=1, source_target_pairs={{0,8},{8,0},{16,24},{24,16},{1,9},{9,1},{17,25},{25,17},{2,10},{10... | collective-permute-start | bytes 11010056 | tf_op jit(solution)/shard_map/ppermute | solution.py:736
  283.1 21.7 %collective-permute-start.12 = (bf16[2,2,32,1536]{3,2,0,1:T(8,128)(2,1)}, bf16[2,2,32,1536]{3,2,0,1:T(8,128)(2,1)}, u32[]{:S(2)}, u32[]{:S(2)}) collective-permute-start(bf16[2,2,32,1536]{3,2,0,1:T(8,128)(2,1)} %fusion.46), channel_id=1, source_target_pairs={{0,16},{8,24},{16,0},{24,8},{1,17},{9,25},{17,1},{25,9},{2,18},{10... | collective-permute-start | bytes 1179656 | tf_op jit(solution)/shard_map/ppermute | solution.py:736
  283.6 21.2 %collective-permute-start.13 = (bf16[2,2,32,1536]{3,2,0,1:T(8,128)(2,1)}, bf16[2,2,32,1536]{3,2,0,1:T(8,128)(2,1)}, u32[]{:S(2)}, u32[]{:S(2)}) collective-permute-start(bf16[2,2,32,1536]{3,2,0,1:T(8,128)(2,1)} %fusion.47), channel_id=1, source_target_pairs={{0,1},{1,0},{2,3},{3,2},{4,5},{5,4},{6,7},{7,6},{8,9},{9,8},{10,11... | collective-permute-start | bytes 1179656 | tf_op jit(solution)/shard_map/ppermute | solution.py:736
  316.8 18.2 %collective-permute-start.15 = (bf16[2,2,2,88,512]{4,3,2,1,0:T(8,128)(2,1)}, bf16[2,2,2,88,512]{4,3,2,1,0:T(8,128)(2,1)S(1)}, u32[]{:S(2)}, u32[]{:S(2)}) collective-permute-start(bf16[2,2,2,88,512]{4,3,2,1,0:T(8,128)(2,1)} %fusion.18), channel_id=1, source_target_pairs={{0,1},{1,0},{2,3},{3,2},{4,5},{5,4},{6,7},{7,6},{8,9},{9,8},{10,11... | collective-permute-start | bytes 2162696 | tf_op jit(solution)/shard_map/ppermute | solution.py:736
  317.4 17.9 %collective-permute-start.16 = (bf16[2,2,2,88,512]{4,3,1,0,2:T(8,128)(2,1)}, bf16[2,2,2,88,512]{4,3,1,0,2:T(8,128)(2,1)S(1)}, u32[]{:S(2)}, u32[]{:S(2)}) collective-permute-start(bf16[2,2,2,88,512]{4,3,1,0,2:T(8,128)(2,1)} %fusion.19), channel_id=1, source_target_pairs={{0,16},{8,24},{16,0},{24,8},{1,17},{9,25},{17,1},{25,9},{2,18},{10... | collective-permute-start | bytes 2162696 | tf_op jit(solution)/shard_map/ppermute | solution.py:736
  336.3 21.6 %collective-permute-start.18 = (bf16[2,2,2,32,1792]{4,3,1,2,0:T(8,128)(2,1)}, bf16[2,2,2,32,1792]{4,3,1,2,0:T(8,128)(2,1)}, u32[]{:S(2)}, u32[]{:S(2)}) collective-permute-start(bf16[2,2,2,32,1792]{4,3,1,2,0:T(8,128)(2,1)} %fusion), channel_id=1, source_target_pairs={{0,1},{1,0},{2,3},{3,2},{4,5},{5,4},{6,7},{7,6},{8,9},{9,8},{10,11... | collective-permute-start | bytes 2752520 | tf_op jit(solution)/shard_map/ppermute | solution.py:736
  337.7 21.1 %collective-permute-start.19 = (bf16[2,2,2,32,1792]{4,3,0,1,2:T(8,128)(2,1)}, bf16[2,2,2,32,1792]{4,3,0,1,2:T(8,128)(2,1)}, u32[]{:S(2)}, u32[]{:S(2)}) collective-permute-start(bf16[2,2,2,32,1792]{4,3,0,1,2:T(8,128)(2,1)} %fusion.1), channel_id=1, source_target_pairs={{0,16},{8,24},{16,0},{24,8},{1,17},{9,25},{17,1},{25,9},{2,18},{10... | collective-permute-start | bytes 2752520 | tf_op jit(solution)/shard_map/ppermute | solution.py:736
  361.1 18.8 %collective-permute-start.21 = (bf16[2,2,32,1792]{3,2,0,1:T(8,128)(2,1)S(1)}, bf16[2,2,32,1792]{3,2,0,1:T(8,128)(2,1)}, u32[]{:S(2)}, u32[]{:S(2)}) collective-permute-start(bf16[2,2,32,1792]{3,2,0,1:T(8,128)(2,1)S(1)} %fusion.36), channel_id=1, source_target_pairs={{0,16},{8,24},{16,0},{24,8},{1,17},{9,25},{17,1},{25,9},{2,18},{10... | collective-permute-start | bytes 1376264 | tf_op jit(solution)/shard_map/ppermute | solution.py:736
  362.0 17.9 %collective-permute-start.22 = (bf16[2,2,32,1792]{3,2,0,1:T(8,128)(2,1)S(1)}, bf16[2,2,32,1792]{3,2,0,1:T(8,128)(2,1)}, u32[]{:S(2)}, u32[]{:S(2)}) collective-permute-start(bf16[2,2,32,1792]{3,2,0,1:T(8,128)(2,1)S(1)} %fusion.37), channel_id=1, source_target_pairs={{0,1},{1,0},{2,3},{3,2},{4,5},{5,4},{6,7},{7,6},{8,9},{9,8},{10,11... | collective-permute-start | bytes 1376264 | tf_op jit(solution)/shard_map/ppermute | solution.py:736
  363.2 15.7 %collective-permute-start.23 = (bf16[2,2,88,512]{3,2,1,0:T(8,128)(2,1)}, bf16[2,2,88,512]{3,2,1,0:T(8,128)(2,1)}, u32[]{:S(2)}, u32[]{:S(2)}) collective-permute-start(bf16[2,2,88,512]{3,2,1,0:T(8,128)(2,1)} %fusion.56), channel_id=1, source_target_pairs={{0,16},{8,24},{16,0},{24,8},{1,17},{9,25},{17,1},{25,9},{2,18},{10... | collective-permute-start | bytes 1081352 | tf_op jit(solution)/shard_map/ppermute | solution.py:736
  364.0 15.9 %collective-permute-start.24 = (bf16[2,2,88,512]{3,2,1,0:T(8,128)(2,1)}, bf16[2,2,88,512]{3,2,1,0:T(8,128)(2,1)}, u32[]{:S(2)}, u32[]{:S(2)}) collective-permute-start(bf16[2,2,88,512]{3,2,1,0:T(8,128)(2,1)} %fusion.57), channel_id=1, source_target_pairs={{0,1},{1,0},{2,3},{3,2},{4,5},{5,4},{6,7},{7,6},{8,9},{9,8},{10,11... | collective-permute-start | bytes 1081352 | tf_op jit(solution)/shard_map/ppermute | solution.py:736
  385.1 23.0 %collective-permute-start.25 = (bf16[2,2,32,1792]{3,2,0,1:T(8,128)(2,1)S(1)}, bf16[2,2,32,1792]{3,2,0,1:T(8,128)(2,1)S(1)}, u32[]{:S(2)}, u32[]{:S(2)}) collective-permute-start(bf16[2,2,32,1792]{3,2,0,1:T(8,128)(2,1)S(1)} %fusion.45), channel_id=1, source_target_pairs={{0,2},{1,3},{2,0},{3,1},{4,6},{5,7},{6,4},{7,5},{8,10},{9,11},{10,... | collective-permute-start | bytes 1376264 | tf_op jit(solution)/shard_map/ppermute | solution.py:736
  385.5 22.6 %collective-permute-start.26 = (bf16[2,2,88,512]{3,2,1,0:T(8,128)(2,1)S(1)}, bf16[2,2,88,512]{3,2,1,0:T(8,128)(2,1)S(1)}, u32[]{:S(2)}, u32[]{:S(2)}) collective-permute-start(bf16[2,2,88,512]{3,2,1,0:T(8,128)(2,1)S(1)} %fusion.65), channel_id=1, source_target_pairs={{0,2},{1,3},{2,0},{3,1},{4,6},{5,7},{6,4},{7,5},{8,10},{9,11},{10,... | collective-permute-start | bytes 1081352 | tf_op jit(solution)/shard_map/ppermute | solution.py:736
  410.2 29.4 %collective-permute-start.33 = (bf16[2,88,512]{2,1,0:T(8,128)(2,1)S(1)}, bf16[2,88,512]{2,1,0:T(8,128)(2,1)S(1)}, u32[]{:S(2)}, u32[]{:S(2)}) collective-permute-start(bf16[2,88,512]{2,1,0:T(8,128)(2,1)S(1)} %dynamic-slice_bitcast_fusion.3), channel_id=1, source_target_pairs={{0,4},{1,5},{2,6},{3,7},{4,0},{5,1},{6,2},{7,3},{8,12},{9,13},{10,... | collective-permute-start | bytes 540680 | tf_op jit(solution)/shard_map/ppermute | solution.py:736
  414.3 15.4 %collective-permute-start.28 = (bf16[2,2,2,32,1152]{4,3,1,2,0:T(8,128)(2,1)S(1)}, bf16[2,2,2,32,1152]{4,3,1,2,0:T(8,128)(2,1)S(1)}, u32[]{:S(2)}, u32[]{:S(2)}) collective-permute-start(bf16[2,2,2,32,1152]{4,3,1,2,0:T(8,128)(2,1)S(1)} %fusion.27), channel_id=1, source_target_pairs={{0,1},{1,0},{2,3},{3,2},{4,5},{5,4},{6,7},{7,6},{8,9},{9,8},{10,11... | collective-permute-start | bytes 1769480 | tf_op jit(solution)/shard_map/ppermute | solution.py:736
  415.3 15.1 %collective-permute-start.29 = (bf16[2,2,2,32,1152]{4,3,0,1,2:T(8,128)(2,1)S(1)}, bf16[2,2,2,32,1152]{4,3,0,1,2:T(8,128)(2,1)S(1)}, u32[]{:S(2)}, u32[]{:S(2)}) collective-permute-start(bf16[2,2,2,32,1152]{4,3,0,1,2:T(8,128)(2,1)S(1)} %fusion.28), channel_id=1, source_target_pairs={{0,16},{8,24},{16,0},{24,8},{1,17},{9,25},{17,1},{25,9},{2,18},{10... | collective-permute-start | bytes 1769480 | tf_op jit(solution)/shard_map/ppermute | solution.py:736
  (45 other events, 260.9 us)
Sparse Core Ops, SparseCore 0:
  29.3 134.8 all-gather.1
